TPU v7x, 256 devices: a whole 4x4x8 slice. The times are simulated.
256 devices in a mesh: dp: 8 (over z), shard: 32 (over x, y, core).
Axes of the slice: x: 4, y: 4, z: 8, core: 2. Of those that a mesh axis runs over, the one named last changes fastest.
Arguments:
- activations: bfloat16 [8192, 8192], P('dp', 'shard'), may hold values from -6 to 6
- cotangent: bfloat16 [8192, 2048], P('dp'), may hold values from -0.0625 to 0.0625
- master: float32 [2048, 8192], P('dp', 'shard'), may hold values from -0.18 to 0.18
- adamw_first_moment: float32 [2048, 8192], P('dp', 'shard'), may hold values from -4 to 4
- second_moment: float32 [2048, 8192], P('dp', 'shard'), may hold values from 0.01 to 1
- new_owner: int32 [8, 1024, 1], P('dp', 'shard'), may hold values from 0 to 27; in each aligned block of 32 rows (0 to 31, 32 to 63, ..., all dimensions but the last counted through in order) at most 2 rows name the same one
Outputs:
- weights: bfloat16 [2048, 8192], P('dp')
- moved_master: float32 [8, 32, 32, 2, 8, 256], P('dp', 'shard')
- moved_first: float32 [8, 32, 32, 2, 8, 256], P('dp', 'shard')
- moved_second: float32 [8, 32, 32, 2, 8, 256], P('dp', 'shard')
Inputs may be any that keep to these rules, and one draw needn't show every extreme that they name: `new_owner`: among the 32 blocks of one data index and one shard index no owner appears more than 2 times, and some owner appears exactly 2 times. Shard indices 28 and above own nothing.
All inputs are finite; a program needn't handle non-finite values.
Results may differ from a plain program's by a relative error of at most 0.007.
Values may be sent and summed in bfloat16 or wider, within the bound.
A program may use at most 64 MiB of HBM per device.

v0:
```python
import jax
import jax.numpy as jnp
from jax import lax
from jax.sharding import PartitionSpec as P

beta_one = 0.9
beta_two = 0.95
learning_rate = 0.003
decay_rate = 0.1
epsilon_value = 1e-08
adam_step = 100


def adam_update(master, adamw_first_moment, second_moment, gradient):
    corr_one = 1.0 - beta_one**adam_step
    corr_two = 1.0 - beta_two**adam_step
    first_new = beta_one * adamw_first_moment + (1.0 - beta_one) * gradient
    second_new = beta_two * second_moment + (1.0 - beta_two) * gradient * gradient
    direction = first_new / corr_one / (jnp.sqrt(second_new / corr_two) + epsilon_value)
    updated_master_weight = master - learning_rate * (direction + decay_rate * master)
    return (updated_master_weight, first_new, second_new)


def shards(activations, cotangent, master, adamw_first_moment, second_moment, new_owner):
    kv_rows, local_cols = master.shape
    gradient = lax.psum_scatter(
        lax.dot_general(
            cotangent, activations, (((0,), (0,)), ((), ())), preferred_element_type=jnp.float32
        ).astype(jnp.bfloat16),
        "dp",
        scatter_dimension=0,
        tiled=True,
    ).astype(jnp.float32)
    owner_ids = new_owner[0, :, 0]
    total_blocks = owner_ids.shape[0]
    rows_per_block = kv_rows // total_blocks
    number_of_shards = lax.axis_size("shard")
    remaining_owners = number_of_shards - number_of_shards // 8
    number_of_slots = max(2, (total_blocks + remaining_owners - 1) // remaining_owners)
    same_owner = owner_ids[:, None] == owner_ids[None, :]
    earlier = lax.broadcasted_iota(
        jnp.int32, (total_blocks, total_blocks), 1
    ) < lax.broadcasted_iota(jnp.int32, (total_blocks, total_blocks), 0)
    slot_rank = jnp.sum(jnp.where(same_owner & earlier, 1, 0), axis=1).astype(jnp.int32)
    dest_iota = lax.broadcasted_iota(
        jnp.int32, (number_of_shards, number_of_slots, total_blocks), 0
    )
    slot_iota = lax.broadcasted_iota(
        jnp.int32, (number_of_shards, number_of_slots, total_blocks), 1
    )
    selector = (
        (owner_ids[None, None, :] == dest_iota) & (slot_rank[None, None, :] == slot_iota)
    ).astype(jnp.float32)

    def pack_slots(values_in):
        blocks = values_in.reshape(total_blocks, rows_per_block * local_cols)
        packed = jnp.einsum("trk,kx->trx", selector, blocks, precision=lax.Precision.HIGHEST)
        return packed.reshape(number_of_shards, number_of_slots, rows_per_block, local_cols)

    updated_master_weight, first_new, second_new = adam_update(
        master, adamw_first_moment, second_moment, gradient
    )
    incoming_rows = (
        lax.all_to_all(
            pack_slots(updated_master_weight), "shard", split_axis=0, concat_axis=0, tiled=True
        ),
        lax.all_to_all(pack_slots(first_new), "shard", split_axis=0, concat_axis=0, tiled=True),
        lax.all_to_all(pack_slots(second_new), "shard", split_axis=0, concat_axis=0, tiled=True),
    )
    relocated = (incoming_rows[0], incoming_rows[1], incoming_rows[2])
    weights = lax.all_gather(
        updated_master_weight.astype(jnp.bfloat16), "shard", axis=1, tiled=True
    )
    out_shape = (1, 1, number_of_shards, number_of_slots, rows_per_block, local_cols)
    return (
        weights,
        relocated[0].reshape(out_shape),
        relocated[1].reshape(out_shape),
        relocated[2].reshape(out_shape),
    )


def solution(mesh):
    in_specs = (
        P("dp", "shard"),
        P("dp", None),
        P("dp", "shard"),
        P("dp", "shard"),
        P("dp", "shard"),
        P("dp", "shard", None),
    )
    out_specs = (
        P("dp", None),
        P("dp", "shard", None, None, None, None),
        P("dp", "shard", None, None, None, None),
        P("dp", "shard", None, None, None, None),
    )
    return jax.shard_map(shards, mesh=mesh, in_specs=in_specs, out_specs=out_specs, check_vma=False)
```

profile of v0, /device:TPU:1, one launch (start us, length us, event | category | flops | bytes accessed | tf_op | source)
XLA Modules:
  0.0 131.4 jit_solution(16757182467101694203)
XLA Ops:
  7.2 0.0 reduce-scatter.2.cloned.1.call-start
  7.3 0.9 copy-done
  8.2 4.5 %convolution_convert_fusion = bf16[2048,256]{1,0:T(8,128)(2,1)} fusion(bf16[1024,2048]{1,0:T(8,128)(2,1)} %param.7, bf16[1024,256]{1,0:T(8,128)(2,1)S(1)} %copy-done), kind=kOutput, calls=%fused_computation | convolution fusion | flops 1074266112 | bytes 5767168 | tf_op jit(solution)/shard_map/dot_general | solution.py:27
  12.7 0.0 all-gather.2.cloned.1.call-start
  12.8 37.6 %reduce-scatter.2.cloned.1.call-done = bf16[256,256]{1,0:T(8,128)(2,1)} async-done(((bf16[2048,256]{1,0:T(8,128)(2,1)}), bf16[256,256]{1,0:T(8,128)(2,1)}) %reduce-scatter.2.cloned.1.call-update) | async-done | bytes 131088 | tf_op jit(solution)/shard_map/reduce_scatter | solution.py:26
  50.4 1.8 %fusion.20 = (bf16[256,256]{1,0:T(8,128)(2,1)}, f32[256,256]{1,0:T(8,128)S(1)}, f32[256,256]{1,0:T(8,128)S(1)}, f32[256,256]{1,0:T(8,128)S(1)}) fusion(f32[256,256]{1,0:T(8,128)S(1)} %copy-done.1, bf16[256,256]{1,0:T(8,128)(2,1)} %reduce-scatter.2.cloned.1.call-done, f32[256,256]{1,0:T(8,128)S(1)} %copy-done.2, f32[256,256]{1,0:T(8,128)S(1)} %copy-done.3), kind=kLoop, calls=%fused_computation.28 | loop fusion | flops 1114112 | bytes 1835008 | tf_op jit(solution)/shard_map/convert_element_type | solution.py:72
  52.2 0.2 select_reduce_fusion
  52.5 0.4 fusion.6
  52.8 1.1 copy.26
  53.9 12.5 %all-to-all-start = ((f32[32,2,8,256]{3,2,1,0:T(8,128)}), f32[32,2,8,256]{3,2,1,0:T(8,128)S(1)}, u32[]{:S(2)}, u32[]{:S(2)}) async-start(f32[32,2,8,256]{3,2,1,0:T(8,128)} %copy.26), calls=%async_computation.1 | async-start | bytes 1048576 | tf_op jit(solution)/shard_map/all_to_all | solution.py:64
  66.5 0.4 fusion.4
  66.8 1.1 copy.28
  67.9 10.8 %all-to-all-done = f32[32,2,8,256]{3,2,1,0:T(8,128)S(1)} async-done(((f32[32,2,8,256]{3,2,1,0:T(8,128)}), f32[32,2,8,256]{3,2,1,0:T(8,128)S(1)}, u32[]{:S(2)}, u32[]{:S(2)}) %all-to-all-start) | async-done | bytes 524320 | tf_op jit(solution)/shard_map/all_to_all | solution.py:64
  78.7 3.7 %all-to-all-start.1 = ((f32[32,2,8,256]{3,2,1,0:T(8,128)}), f32[32,2,8,256]{3,2,1,0:T(8,128)S(1)}, u32[]{:S(2)}, u32[]{:S(2)}) async-start(f32[32,2,8,256]{3,2,1,0:T(8,128)} %copy.28), calls=%async_computation.2 | async-start | bytes 1048576 | tf_op jit(solution)/shard_map/all_to_all | solution.py:67
  82.5 0.4 fusion.2
  82.8 1.1 copy.30
  83.9 10.1 %all-to-all-done.1 = f32[32,2,8,256]{3,2,1,0:T(8,128)S(1)} async-done(((f32[32,2,8,256]{3,2,1,0:T(8,128)}), f32[32,2,8,256]{3,2,1,0:T(8,128)S(1)}, u32[]{:S(2)}, u32[]{:S(2)}) %all-to-all-start.1) | async-done | bytes 524320 | tf_op jit(solution)/shard_map/all_to_all | solution.py:67
  94.0 3.7 %all-to-all-start.2 = ((f32[32,2,8,256]{3,2,1,0:T(8,128)}), f32[32,2,8,256]{3,2,1,0:T(8,128)S(1)}, u32[]{:S(2)}, u32[]{:S(2)}) async-start(f32[32,2,8,256]{3,2,1,0:T(8,128)} %copy.30), calls=%async_computation.3 | async-start | bytes 1048576 | tf_op jit(solution)/shard_map/all_to_all | solution.py:68
  97.7 14.2 %all-to-all-done.2 = f32[32,2,8,256]{3,2,1,0:T(8,128)S(1)} async-done(((f32[32,2,8,256]{3,2,1,0:T(8,128)}), f32[32,2,8,256]{3,2,1,0:T(8,128)S(1)}, u32[]{:S(2)}, u32[]{:S(2)}) %all-to-all-start.2) | async-done | bytes 524320 | tf_op jit(solution)/shard_map/all_to_all | solution.py:68
  111.8 5.7 %all-gather.2.cloned.1.call-done = bf16[256,8192]{1,0:T(8,128)(2,1)} async-done(((bf16[256,256]{1,0:T(8,128)(2,1)}), bf16[256,8192]{1,0:T(8,128)(2,1)}) %all-gather.2.cloned.1.call-update) | async-done | bytes 4194320 | tf_op jit(solution)/shard_map/all_gather | solution.py:71
  117.5 4.6 %copy.51 = bf16[256,8192]{1,0:T(8,128)(2,1)} copy(bf16[256,8192]{1,0:T(8,128)(2,1)} %all-gather.2.cloned.1.call-done) | data formatting | bytes 8388608
  122.1 0.8 copy.52
  122.9 0.8 copy.53
  123.7 0.8 copy.54
  (14 shorter events, 0.2 us)
Async XLA Ops:
  7.2 1.0 copy-start
  7.2 43.2 %copy-start.1 = (f32[256,256]{1,0:T(8,128)S(1)}, f32[256,256]{1,0:T(8,128)}, u32[]{:S(2)}) copy-start(f32[256,256]{1,0:T(8,128)} %param.8) | copy-start | bytes 786436
  7.2 43.2 %copy-start.2 = (f32[256,256]{1,0:T(8,128)S(1)}, f32[256,256]{1,0:T(8,128)}, u32[]{:S(2)}) copy-start(f32[256,256]{1,0:T(8,128)} %param.9) | copy-start | bytes 786436
  7.2 43.2 %copy-start.3 = (f32[256,256]{1,0:T(8,128)S(1)}, f32[256,256]{1,0:T(8,128)}, u32[]{:S(2)}) copy-start(f32[256,256]{1,0:T(8,128)} %param.10) | copy-start | bytes 786436
  7.2 45.0 %copy-start.4 = (s32[1,32,1]{1,2,0:T(1,128)S(1)}, s32[1,32,1]{1,2,0:T(1,128)}, u32[]{:S(2)}) copy-start(s32[1,32,1]{1,2,0:T(1,128)} %param.11) | copy-start | bytes 388
  7.2 43.2 %reduce-scatter.2.cloned.1.call-start = ((), (), s32[]{:S(2)}) async-start(), calls=%async_computation.4 | async-start | bytes 1179648 | tf_op jit(solution)/shard_map/reduce_scatter | solution.py:26
  12.7 104.8 %all-gather.2.cloned.1.call-start = ((), (), s32[]{:S(2)}) async-start(), calls=%async_computation.5 | async-start | bytes 4325376 | tf_op jit(solution)/shard_map/all_gather | solution.py:71
  53.9 24.8 %all-to-all-start = ((f32[32,2,8,256]{3,2,1,0:T(8,128)}), f32[32,2,8,256]{3,2,1,0:T(8,128)S(1)}, u32[]{:S(2)}, u32[]{:S(2)}) async-start(f32[32,2,8,256]{3,2,1,0:T(8,128)} %copy.26), calls=%async_computation.1 | async-start | bytes 1048576 | tf_op jit(solution)/shard_map/all_to_all | solution.py:64
  78.7 15.3 %all-to-all-start.1 = ((f32[32,2,8,256]{3,2,1,0:T(8,128)}), f32[32,2,8,256]{3,2,1,0:T(8,128)S(1)}, u32[]{:S(2)}, u32[]{:S(2)}) async-start(f32[32,2,8,256]{3,2,1,0:T(8,128)} %copy.28), calls=%async_computation.2 | async-start | bytes 1048576 | tf_op jit(solution)/shard_map/all_to_all | solution.py:67
  94.0 17.8 %all-to-all-start.2 = ((f32[32,2,8,256]{3,2,1,0:T(8,128)}), f32[32,2,8,256]{3,2,1,0:T(8,128)S(1)}, u32[]{:S(2)}, u32[]{:S(2)}) async-start(f32[32,2,8,256]{3,2,1,0:T(8,128)} %copy.30), calls=%async_computation.3 | async-start | bytes 1048576 | tf_op jit(solution)/shard_map/all_to_all | solution.py:68
Sparse Core Ops, SparseCore 0:
  12.8 37.5 reduce-scatter.1
  53.4 64.0 all-gather.1
where the time goes:
time: 132 us; the launch traced here: 131 us
  waiting for transfers between devices  78.4 us (59%)
  starting transfers between devices  19.9 us (15%)
  between operations  14.2 us (11%)
  local copies, waits for them, and re-layouts  11.4 us (9%)
  matrix products  5.56 us (4%)
  other arithmetic  1.97 us (1%)
    reduce_scatter x1, waiting for transfers between devices, shards(): lax.psum_scatter(lax.dot_general(cotangent, activations, (((0,), (0,)), (...  37.6 us
    all_to_all x1, waiting for transfers between devices, shards(): lax.all_to_all(pack_slots(second_new), 'shard', split_axis=0, concat_axis...  14.2 us
    all_to_all x1, starting transfers between devices, shards(): lax.all_to_all(pack_slots(updated_master_weight), 'shard', split_axis=0,...  12.5 us
    all_to_all x1, waiting for transfers between devices, shards(): lax.all_to_all(pack_slots(updated_master_weight), 'shard', split_axis=0,...  10.8 us
    all_to_all x1, waiting for transfers between devices, shards(): lax.all_to_all(pack_slots(first_new), 'shard', split_axis=0, concat_axis=...  10.1 us
    unnamed x14, local copies, waits for them, and re-layouts  7.99 us
    all_gather x1, waiting for transfers between devices, shards(): lax.all_gather(updated_master_weight.astype(jnp.bfloat16), 'shard', axis=...  5.68 us
    dot_general x1, matrix products, shards(): lax.dot_general(cotangent, activations, (((0,), (0,)), ((), ())), preferr...  4.49 us
  transfers between devices with their start and end apart: 5, of which 5 were waited for; matrix products, arithmetic and copies ran while one was open for 4% of the time, Pallas kernels for 0%

commit v1 on v0

v1 whole, which is shorter than its diff:
```python
import functools

import jax
import jax.numpy as jnp
from jax import lax
from jax.experimental import pallas as pl
from jax.experimental.pallas import tpu as pltpu
from jax.sharding import PartitionSpec as P

beta_one = 0.9
beta_two = 0.95
learning_rate = 0.003
decay_rate = 0.1
epsilon_value = 1e-08
adam_step = 100

MESH = pl.DeviceIdType.MESH
BF16 = jnp.bfloat16
F32 = jnp.float32

NZ = 8
NS = 32
OWNERS = 28
SLOT_ROWS = 16
C = 256
SUBS = 2
R = C // SUBS
H = R // 2


def adam_update(master, adamw_first_moment, second_moment, gradient):
    corr_one = 1.0 - beta_one**adam_step
    corr_two = 1.0 - beta_two**adam_step
    first_new = beta_one * adamw_first_moment + (1.0 - beta_one) * gradient
    second_new = beta_two * second_moment + (1.0 - beta_two) * gradient * gradient
    direction = first_new / corr_one / (jnp.sqrt(second_new / corr_two) + epsilon_value)
    updated_master_weight = master - learning_rate * (direction + decay_rate * master)
    return (updated_master_weight, first_new, second_new)


def exchange_kernel(
    act_hbm, cot_hbm, mas_hbm, fir_hbm, sec_hbm, own_ref,
    w_ref, out_mas, out_fir, out_sec,
    act, cot, mas, fir, sec, load_sem,
    pick, st_send, st_recv, g_send, g_recv,
    far_send, far_recv, mid_send, mid_recv, near_send, near_recv, two_send, two_recv,
    keep, grad,
    rs_send_sem, rs_recv_sem, ag_send_sem, ag_recv_sem, ag_half_sem, sib_sem,
    st_send_sem, st_recv_sem, g_send_sem, g_recv_sem,
):
    z = lax.axis_index("dp")
    me = lax.axis_index("shard")
    core = lax.rem(me, 2)
    y = lax.rem(lax.div(me, 2), 4)
    x = lax.div(me, 8)

    def at_z(step):
        return lax.rem(z + step + NZ, NZ)

    def plane(dx, dy, dc=0):
        return (lax.rem(x + dx + 4, 4) * 4 + lax.rem(y + dy + 4, 4)) * 2 + lax.rem(core + dc, 2)

    sibling = plane(0, 0, 1)

    order = (4, 3, 5, 1, 7, 2, 6, 0)
    loads = [pltpu.make_async_copy(act_hbm, act, load_sem.at[0])]
    cot_loads = {}
    for r in order:
        start = pl.multiple_of(at_z(r) * C, C)
        cot_loads[r] = pltpu.make_async_copy(
            cot_hbm.at[:, pl.ds(start, C)], cot.at[r], load_sem.at[1 + r]
        )
    state_loads = [
        pltpu.make_async_copy(mas_hbm, mas, load_sem.at[9]),
        pltpu.make_async_copy(fir_hbm, fir, load_sem.at[10]),
        pltpu.make_async_copy(sec_hbm, sec, load_sem.at[11]),
    ]
    loads[0].start()
    for r in order[:3]:
        cot_loads[r].start()
    for r in order[3:]:
        cot_loads[r].start()
    for load in state_loads:
        load.start()

    barrier = pltpu.get_barrier_semaphore()
    for step in (1, -1, 2, -2):
        pl.semaphore_signal(barrier, inc=1, device_id=(at_z(step), me), device_id_type=MESH)

    @pl.loop(1, NS)
    def _(i):
        pl.semaphore_signal(
            barrier, inc=1, device_id=(z, lax.rem(me + i, NS)), device_id_type=MESH
        )

    def partial(r):
        cot_loads[r].wait()
        return lax.dot_general(
            cot[r], act[...], (((0,), (0,)), ((), ())), preferred_element_type=F32
        )

    loads[0].wait()
    part = partial(4)
    far_send[...] = part.astype(BF16)
    mid_send[0] = partial(3).astype(BF16)
    mid_send[1] = partial(5).astype(BF16)

    pl.semaphore_wait(barrier, NS - 1 + 4)

    rs_sends = []

    def rs_copy(src, dst, index, step):
        copy = pltpu.make_async_remote_copy(
            src_ref=src, dst_ref=dst, send_sem=rs_send_sem.at[index], recv_sem=rs_recv_sem.at[index],
            device_id=(at_z(step), me), device_id_type=MESH,
        )
        return copy

    def far(sub, way):
        rows = pl.ds(sub * R + way * H, H)
        slot = pl.ds(sub * H, H)
        return rs_copy(far_send.at[rows], far_recv.at[way, slot], (sub * 4 + 0) * 2 + way, 2 - 4 * way)

    def mid(sub, way):
        rows = pl.ds(sub * R, R)
        return rs_copy(mid_send.at[way, rows], mid_recv.at[way, rows], (sub * 4 + 1) * 2 + way, 1 - 2 * way)

    def near(sub, way):
        rows = pl.ds(sub * R, R)
        return rs_copy(near_send.at[way, rows], near_recv.at[way, rows], (sub * 4 + 2) * 2 + way, 1 - 2 * way)

    def two(sub, way):
        rows = pl.ds(sub * R, R)
        return rs_copy(two_send.at[way, rows], two_recv.at[way, rows], (sub * 4 + 3) * 2 + way, 2 - 4 * way)

    def rs_start(copy):
        copy.start()
        rs_sends.append(copy)

    for sub in range(SUBS):
        for way in (0, 1):
            rs_start(far(sub, way))
            rs_start(mid(sub, way))

    keep[1] = partial(2)
    keep[2] = partial(6)
    near_send[0] = partial(1).astype(BF16)
    near_send[1] = partial(7).astype(BF16)
    for sub in range(SUBS):
        for way in (0, 1):
            rs_start(near(sub, way))
    keep[0] = partial(0)

    owner = own_ref[...].astype(F32)
    row_id = lax.broadcasted_iota(jnp.int32, (NS, NS), 0)
    col_id = lax.broadcasted_iota(jnp.int32, (NS, NS), 1)
    wide = jnp.broadcast_to(owner, (NS, NS))
    tall = jnp.sum(jnp.where(row_id == col_id, wide, 0.0), axis=1, keepdims=True)
    rank = jnp.sum(jnp.where((wide == tall) & (row_id < col_id), 1.0, 0.0), axis=0, keepdims=True)
    key = jnp.broadcast_to(owner * 2.0 + rank, (16, NS)).astype(BF16)
    spread = lax.broadcasted_iota(jnp.int32, (NS, C), 0) == lax.div(
        lax.broadcasted_iota(jnp.int32, (NS, C), 1), 8
    )
    slot_of = jnp.dot(key, spread.astype(F32).astype(BF16), preferred_element_type=F32)[0:1]
    within = lax.rem(lax.broadcasted_iota(jnp.int32, (1, C), 1), 8).astype(F32)
    target_row = slot_of * 8.0 + within
    slot_row = lax.broadcasted_iota(jnp.int32, (OWNERS * SLOT_ROWS, C), 0).astype(F32)
    pick[...] = jnp.where(slot_row == target_row, 1.0, 0.0).astype(BF16)

    for load in state_loads:
        load.wait()

    def packed(values):
        return (
            jnp.dot(pick[...], values, preferred_element_type=F32)
            .astype(BF16)
            .reshape(OWNERS, SLOT_ROWS, C)
        )

    st_send[:, 0] = packed(mas[...].astype(BF16))
    st_send[:, 1] = packed(fir[...].astype(BF16))
    st_send[:, 2] = packed(sec[...].astype(BF16))

    def st_copy(owner_id):
        return pltpu.make_async_remote_copy(
            src_ref=st_send.at[owner_id], dst_ref=st_recv.at[me],
            send_sem=st_send_sem.at[owner_id], recv_sem=st_recv_sem.at[me],
            device_id=(z, owner_id), device_id_type=MESH,
        )

    def g_copy(owner_id):
        return pltpu.make_async_remote_copy(
            src_ref=g_send.at[owner_id], dst_ref=g_recv.at[me],
            send_sem=g_send_sem.at[owner_id], recv_sem=g_recv_sem.at[me],
            device_id=(z, owner_id), device_id_type=MESH,
        )

    def to_owners(make, act_on):
        @pl.loop(1, NS)
        def _(i):
            owner_id = lax.rem(me + i, NS)

            @pl.when(owner_id < OWNERS)
            def _():
                act_on(make(owner_id))

    to_owners(st_copy, lambda copy: copy.start())

    for sub in range(SUBS):
        rows = pl.ds(sub * R, R)
        for way in (0, 1):
            far(sub, way).wait_recv()
            mid(sub, way).wait_recv()
            half = pl.ds(sub * R + way * H, H)
            keep[1 + way, rows] = keep[1 + way, rows] + mid_recv[way, rows].astype(F32)
            keep[1 + way, half] = keep[1 + way, half] + far_recv[way, pl.ds(sub * H, H)].astype(F32)
            two_send[way, rows] = keep[1 + way, rows].astype(BF16)
            rs_start(two(sub, way))

    ag_sends = []

    def ag_copy(sub, source, dx, dy, first=0, count=R, recv_sem=None):
        part_of = w_ref.at[source, pl.ds(sub * R + first, count)]
        copy = pltpu.make_async_remote_copy(
            src_ref=part_of, dst_ref=part_of,
            send_sem=ag_send_sem.at[len(ag_sends)],
            recv_sem=ag_recv_sem.at[sub, source] if recv_sem is None else recv_sem,
            device_id=(z, plane(dx, dy)), device_id_type=MESH,
        )
        copy.start()
        ag_sends.append(copy)

    def to_sibling(sub, source):
        part_of = w_ref.at[source, pl.ds(sub * R, R)]
        copy = pltpu.make_async_remote_copy(
            src_ref=part_of, dst_ref=part_of,
            send_sem=ag_send_sem.at[len(ag_sends)], recv_sem=sib_sem.at[sub, source],
            device_id=(z, sibling), device_id_type=MESH,
        )
        copy.start()
        ag_sends.append(copy)

    def arrived(sub, source, sem, first=0, count=R):
        part_of = w_ref.at[source, pl.ds(sub * R + first, count)]
        pltpu.make_async_remote_copy(
            src_ref=part_of, dst_ref=part_of, send_sem=sem, recv_sem=sem,
            device_id=(z, sibling), device_id_type=MESH,
        ).wait_recv()

    def update(sub):
        rows = pl.ds(sub * R, R)
        for way in (0, 1):
            near(sub, way).wait_recv()
            two(sub, way).wait_recv()
        total = keep[0, rows]
        for way in (0, 1):
            total = total + near_recv[way, rows].astype(F32) + two_recv[way, rows].astype(F32)
        new_master, _, _ = adam_update(mas[rows], fir[rows], sec[rows], total)
        w_ref[me, rows] = new_master.astype(BF16)
        grad[rows] = total.astype(BF16)
        for dx, dy in ((1, 0), (-1, 0), (0, 1), (0, -1), (2, 0), (0, 2)):
            ag_copy(sub, me, dx, dy)
        to_sibling(sub, me)

    def forward(sub):
        for (dx, dy), onward in (
            ((-1, 0), ((0, 1),)),
            ((1, 0), ((0, -1),)),
            ((0, -1), ((-1, 0),)),
            ((0, 1), ((1, 0),)),
        ):
            source = plane(dx, dy)
            arrived(sub, source, ag_recv_sem.at[sub, source])
            for to in onward:
                ag_copy(sub, source, *to)
            to_sibling(sub, source)
        source = plane(2, 0)
        arrived(sub, source, ag_recv_sem.at[sub, source])
        ag_copy(sub, source, 0, 2, 0, H, ag_half_sem.at[sub, 0])
        ag_copy(sub, source, 0, 1)
        ag_copy(sub, source, 0, -1)
        to_sibling(sub, source)
        source = plane(0, 2)
        arrived(sub, source, ag_recv_sem.at[sub, source])
        ag_copy(sub, source, 2, 0, H, H, ag_half_sem.at[sub, 1])
        ag_copy(sub, source, 1, 0)
        ag_copy(sub, source, -1, 0)
        to_sibling(sub, source)

    def finish(sub):
        for dx, dy in ((1, 1), (1, -1), (-1, 1), (-1, -1), (2, 1), (2, -1), (1, 2), (-1, 2)):
            source = plane(dx, dy)
            arrived(sub, source, ag_recv_sem.at[sub, source])
            to_sibling(sub, source)
        source = plane(2, 2)
        arrived(sub, source, ag_half_sem.at[sub, 0], 0, H)
        arrived(sub, source, ag_half_sem.at[sub, 1], H, H)
        to_sibling(sub, source)

    for sub in range(SUBS):
        update(sub)
        if sub < SUBS - 1:
            forward(sub)
        if sub >= 1:
            finish(sub - 1)

    g_send[...] = packed(grad[...])
    to_owners(g_copy, lambda copy: copy.start())
    forward(SUBS - 1)

    @pl.when(me < OWNERS)
    def _():
        st_recv[me] = st_send[me]
        g_recv[me] = g_send[me]

        @pl.loop(0, NS)
        def _(source):
            @pl.when(source != me)
            def _():
                for buffer, sem in ((st_recv, st_recv_sem), (g_recv, g_recv_sem)):
                    pltpu.make_async_remote_copy(
                        src_ref=buffer.at[source], dst_ref=buffer.at[source],
                        send_sem=sem.at[source], recv_sem=sem.at[source],
                        device_id=(z, sibling), device_id_type=MESH,
                    ).wait_recv()

            new_master, new_first, new_second = adam_update(
                st_recv[source, 0].astype(F32),
                st_recv[source, 1].astype(F32),
                st_recv[source, 2].astype(F32),
                g_recv[source].astype(F32),
            )
            out_mas[source] = new_master
            out_fir[source] = new_first
            out_sec[source] = new_second

    @pl.when(me >= OWNERS)
    def _():
        for out in (out_mas, out_fir, out_sec):
            out[...] = jnp.zeros_like(out)

    finish(SUBS - 1)

    for sub in range(SUBS):
        for dx in range(4):
            for dy in range(4):
                source = plane(dx, dy, 1)
                arrived(sub, source, sib_sem.at[sub, source])
    for copy in rs_sends + ag_sends:
        copy.wait_send()
    to_owners(st_copy, lambda copy: copy.wait_send())
    to_owners(g_copy, lambda copy: copy.wait_send())


def store_kernel(w_ref, mas_ref, fir_ref, sec_ref, weights, out_mas, out_fir, out_sec, sem):
    copies = [
        pltpu.make_async_copy(w_ref.at[s], weights.at[:, pl.ds(s * C, C)], sem.at[s])
        for s in range(NS)
    ]
    copies.append(pltpu.make_async_copy(mas_ref, out_mas, sem.at[NS]))
    copies.append(pltpu.make_async_copy(fir_ref, out_fir, sem.at[NS + 1]))
    copies.append(pltpu.make_async_copy(sec_ref, out_sec, sem.at[NS + 2]))
    for copy in copies:
        copy.start()
    for copy in copies:
        copy.wait()


def shards(activations, cotangent, master, adamw_first_moment, second_moment, new_owner):
    tokens = activations.shape[0]
    moved = (NS, SLOT_ROWS, C)
    hbm = pl.BlockSpec(memory_space=pl.ANY)
    vmem = pl.BlockSpec(memory_space=pltpu.VMEM)
    dma = pltpu.SemaphoreType.DMA
    gathered, mas, fir, sec = pl.pallas_call(
        exchange_kernel,
        out_shape=(
            pltpu.VMEM((NS, C, C), BF16),
            pltpu.VMEM(moved, F32),
            pltpu.VMEM(moved, F32),
            pltpu.VMEM(moved, F32),
        ),
        in_specs=[hbm] * 5 + [vmem],
        out_specs=[vmem] * 4,
        scratch_shapes=[
            pltpu.VMEM((tokens, C), BF16),
            pltpu.VMEM((NZ, tokens, C), BF16),
            pltpu.VMEM((C, C), F32),
            pltpu.VMEM((C, C), F32),
            pltpu.VMEM((C, C), F32),
            dma((12,)),
            pltpu.VMEM((OWNERS * SLOT_ROWS, C), BF16),
            pltpu.VMEM((OWNERS, 3, SLOT_ROWS, C), BF16),
            pltpu.VMEM((NS, 3, SLOT_ROWS, C), BF16),
            pltpu.VMEM((OWNERS, SLOT_ROWS, C), BF16),
            pltpu.VMEM((NS, SLOT_ROWS, C), BF16),
            pltpu.VMEM((C, C), BF16),
            pltpu.VMEM((2, C // 2, C), BF16),
            pltpu.VMEM((2, C, C), BF16),
            pltpu.VMEM((2, C, C), BF16),
            pltpu.VMEM((2, C, C), BF16),
            pltpu.VMEM((2, C, C), BF16),
            pltpu.VMEM((2, C, C), BF16),
            pltpu.VMEM((2, C, C), BF16),
            pltpu.VMEM((3, C, C), F32),
            pltpu.VMEM((C, C), BF16),
            dma((SUBS * 8,)),
            dma((SUBS * 8,)),
            dma((SUBS * 32,)),
            dma((SUBS, NS)),
            dma((SUBS, 2)),
            dma((SUBS, NS)),
            dma((NS,)),
            dma((NS,)),
            dma((NS,)),
            dma((NS,)),
        ],
        compiler_params=pltpu.CompilerParams(
            collective_id=0, has_side_effects=True, vmem_limit_bytes=40 * 2**20
        ),
        name="exchange",
    )(
        activations, cotangent, master, adamw_first_moment, second_moment,
        new_owner.reshape(1, NS),
    )
    weights, mas, fir, sec = pl.pallas_call(
        store_kernel,
        out_shape=(
            jax.ShapeDtypeStruct((C, NS * C), BF16),
            jax.ShapeDtypeStruct(moved, F32),
            jax.ShapeDtypeStruct(moved, F32),
            jax.ShapeDtypeStruct(moved, F32),
        ),
        in_specs=[vmem] * 4,
        out_specs=[hbm] * 4,
        scratch_shapes=[dma((NS + 3,))],
        name="store",
    )(gathered, mas, fir, sec)
    out_shape = (1, 1, NS, 2, SLOT_ROWS // 2, C)
    return (weights, mas.reshape(out_shape), fir.reshape(out_shape), sec.reshape(out_shape))


def solution(mesh):
    in_specs = (
        P("dp", "shard"),
        P("dp", None),
        P("dp", "shard"),
        P("dp", "shard"),
        P("dp", "shard"),
        P("dp", "shard", None),
    )
    out_specs = (
        P("dp", None),
        P("dp", "shard", None, None, None, None),
        P("dp", "shard", None, None, None, None),
        P("dp", "shard", None, None, None, None),
    )
    return jax.shard_map(shards, mesh=mesh, in_specs=in_specs, out_specs=out_specs, check_vma=False)
```

time: 132 us -> 69.3 us (0.53)
  waiting for transfers between devices: 78.4 us -> 0 us
  Pallas kernels: 0 us -> 57.2 us
  starting transfers between devices: 19.9 us -> 0 us
  between operations: 14.2 us -> 0.67 us
  matrix products: 5.56 us -> 0 us
  other arithmetic: 1.97 us -> 0 us
    pallas_call x0 -> x2, Pallas kernels: none -> 57.2 us  [the longest x1 51.8 us: shards(): pl.pallas_call(exchange_kernel, out_shape=(pltpu.VMEM((NS, C, C), BF16),...]
    reduce_scatter x1 -> x0, waiting for transfers between devices: 37.6 us -> none  [shards(): lax.psum_scatter(lax.dot_general(cotangent, activations, (((0,), (0,)), (...]
    all_to_all x3 -> x0, waiting for transfers between devices: 35 us -> none  [the longest x1 14.2 us: shards(): lax.all_to_all(pack_slots(second_new), 'shard', split_axis=0, concat_axis...]
    all_to_all x3 -> x0, starting transfers between devices: 19.8 us -> none  [the longest x1 12.5 us: shards(): lax.all_to_all(pack_slots(updated_master_weight), 'shard', split_axis=0,...]
    all_gather x1 -> x0, waiting for transfers between devices: 5.68 us -> none  [shards(): lax.all_gather(updated_master_weight.astype(jnp.bfloat16), 'shard', axis=...]
    dot_general x4 -> x0, matrix products: 5.56 us -> none  [the longest x1 4.49 us: shards(): lax.dot_general(cotangent, activations, (((0,), (0,)), ((), ())), preferr...]
    dot_general x3 -> x0, local copies, waits for them, and re-layouts: 3.3 us -> none  [pack_slots(): jnp.einsum('trk,kx->trx', selector, blocks, precision=lax.Precision.HIGHEST)]
    unnamed x14 -> x20, local copies, waits for them, and re-layouts: 7.99 us -> 11.1 us
  transfers between devices with their start and end apart: 5 -> 0, of which waited for: 5 -> 0; matrix products, arithmetic and copies ran while one was open for 4% -> 0% of each run, Pallas kernels for 0% -> 0%
where the time goes in v1:
time: 69.3 us; the launch traced here: 69 us
  Pallas kernels  57.2 us (83%)
  local copies, waits for them, and re-layouts  11.1 us (16%)
    pallas_call x1, Pallas kernels, shards(): pl.pallas_call(exchange_kernel, out_shape=(pltpu.VMEM((NS, C, C), BF16),...  51.8 us
    unnamed x20, local copies, waits for them, and re-layouts  11.1 us
    pallas_call x1, Pallas kernels, shards(): pl.pallas_call(store_kernel, out_shape=(jax.ShapeDtypeStruct((C, NS * C),...  5.4 us

profile of v1, /device:TPU:1, one launch (start us, length us, event | category | flops | bytes accessed | tf_op | source)
XLA Modules:
  0.0 69.0 jit_solution(4088955883360756168)
XLA Ops:
  0.6 0.0 copy-start
  0.6 2.2 %copy-done = bf16[1024,2048]{1,0:T(8,128)(2,1)S(1)} copy-done((bf16[1024,2048]{1,0:T(8,128)(2,1)S(1)}, bf16[1024,2048]{1,0:T(8,128)(2,1)}, u32[]{:S(2)}) %copy-start) | copy-done | bytes 4194328
  2.8 0.0 copy-start.2
  2.8 1.0 %copy-done.2 = bf16[1024,256]{1,0:T(8,128)(2,1)S(1)} copy-done((bf16[1024,256]{1,0:T(8,128)(2,1)S(1)}, bf16[1024,256]{1,0:T(8,128)(2,1)}, u32[]{:S(2)}) %copy-start.2) | copy-done | bytes 524312
  3.9 0.0 copy-start.6
  3.9 0.9 %copy-done.6 = f32[256,256]{1,0:T(8,128)S(1)} copy-done((f32[256,256]{1,0:T(8,128)S(1)}, f32[256,256]{1,0:T(8,128)}, u32[]{:S(2)}) %copy-start.6) | copy-done | bytes 262168
  4.8 0.0 copy-start.7
  4.8 0.9 %copy-done.7 = f32[256,256]{1,0:T(8,128)S(1)} copy-done((f32[256,256]{1,0:T(8,128)S(1)}, f32[256,256]{1,0:T(8,128)}, u32[]{:S(2)}) %copy-start.7) | copy-done | bytes 262168
  5.8 0.0 copy-start.8
  5.8 0.9 %copy-done.8 = f32[256,256]{1,0:T(8,128)S(1)} copy-done((f32[256,256]{1,0:T(8,128)S(1)}, f32[256,256]{1,0:T(8,128)}, u32[]{:S(2)}) %copy-start.8) | copy-done | bytes 262168
  6.7 0.0 copy-start.9
  6.7 0.7 copy-done.9
  7.4 51.8 %exchange.1 = (bf16[32,256,256]{2,1,0:T(8,128)(2,1)S(1)}, f32[32,16,256]{2,1,0:T(8,128)S(1)}, f32[32,16,256]{2,1,0:T(8,128)S(1)}, f32[32,16,256]{2,1,0:T(8,128)S(1)}) custom-call(bf16[1024,256]{1,0:T(8,128)(2,1)S(1)} %copy-done.2, bf16[1024,2048]{1,0:T(8,128)(2,1)S(1)} %copy-done, f32[256,256]{1,0:T(8,128)S(1)} %copy-done.6, f32[256,256]{1,0:T(8,128)S(1)} %copy-done.7, ...), custom_call_target="tpu_custom_call" | custom-call | tf_op jit(solution)/shard_map/exchange/pallas_call | solution.py:375
  59.2 0.0 copy-start.1
  59.2 1.9 %copy-done.1 = bf16[32,256,256]{2,1,0:T(8,128)(2,1)} copy-done((bf16[32,256,256]{2,1,0:T(8,128)(2,1)}, bf16[32,256,256]{2,1,0:T(8,128)(2,1)S(1)}, u32[]{:S(2)}) %copy-start.1) | copy-done | bytes 4194328
  61.2 0.0 copy-start.3
  61.2 0.8 %copy-done.3 = f32[32,16,256]{2,1,0:T(8,128)} copy-done((f32[32,16,256]{2,1,0:T(8,128)}, f32[32,16,256]{2,1,0:T(8,128)S(1)}, u32[]{:S(2)}) %copy-start.3) | copy-done | bytes 524312
  62.0 0.0 copy-start.4
  62.0 0.8 %copy-done.4 = f32[32,16,256]{2,1,0:T(8,128)} copy-done((f32[32,16,256]{2,1,0:T(8,128)}, f32[32,16,256]{2,1,0:T(8,128)S(1)}, u32[]{:S(2)}) %copy-start.4) | copy-done | bytes 524312
  62.8 0.0 copy-start.5
  62.8 0.8 %copy-done.5 = f32[32,16,256]{2,1,0:T(8,128)} copy-done((f32[32,16,256]{2,1,0:T(8,128)}, f32[32,16,256]{2,1,0:T(8,128)S(1)}, u32[]{:S(2)}) %copy-start.5) | copy-done | bytes 524312
  63.6 5.4 %store.1 = (bf16[256,8192]{1,0:T(8,128)(2,1)}, f32[32,16,256]{2,1,0:T(8,128)}, f32[32,16,256]{2,1,0:T(8,128)}, f32[32,16,256]{2,1,0:T(8,128)}) custom-call(bf16[32,256,256]{2,1,0:T(8,128)(2,1)} %copy-done.1, f32[32,16,256]{2,1,0:T(8,128)} %copy-done.3, f32[32,16,256]{2,1,0:T(8,128)} %copy-done.4, f32[32,16,256]{2,1,0:T(8,128)} %copy-done.5), custom_call_target="tpu_custom_call" | custom-call | tf_op jit(solution)/shard_map/store/pallas_call | solution.py:426
Async XLA Ops:
  0.6 2.2 %copy-start = (bf16[1024,2048]{1,0:T(8,128)(2,1)S(1)}, bf16[1024,2048]{1,0:T(8,128)(2,1)}, u32[]{:S(2)}) copy-start(bf16[1024,2048]{1,0:T(8,128)(2,1)} %cot_hbm.1) | copy-start | bytes 12582916
  2.8 1.0 %copy-start.2 = (bf16[1024,256]{1,0:T(8,128)(2,1)S(1)}, bf16[1024,256]{1,0:T(8,128)(2,1)}, u32[]{:S(2)}) copy-start(bf16[1024,256]{1,0:T(8,128)(2,1)} %act_hbm.1) | copy-start | bytes 1572868
  3.9 0.9 %copy-start.6 = (f32[256,256]{1,0:T(8,128)S(1)}, f32[256,256]{1,0:T(8,128)}, u32[]{:S(2)}) copy-start(f32[256,256]{1,0:T(8,128)} %mas_hbm.1) | copy-start | bytes 786436
  4.8 0.9 %copy-start.7 = (f32[256,256]{1,0:T(8,128)S(1)}, f32[256,256]{1,0:T(8,128)}, u32[]{:S(2)}) copy-start(f32[256,256]{1,0:T(8,128)} %fir_hbm.1) | copy-start | bytes 786436
  5.8 0.9 %copy-start.8 = (f32[256,256]{1,0:T(8,128)S(1)}, f32[256,256]{1,0:T(8,128)}, u32[]{:S(2)}) copy-start(f32[256,256]{1,0:T(8,128)} %sec_hbm.1) | copy-start | bytes 786436
  6.7 0.7 copy-start.9
  59.2 2.0 %copy-start.1 = (bf16[32,256,256]{2,1,0:T(8,128)(2,1)}, bf16[32,256,256]{2,1,0:T(8,128)(2,1)S(1)}, u32[]{:S(2)}) copy-start(bf16[32,256,256]{2,1,0:T(8,128)(2,1)S(1)} %get-tuple-element.12.w_ref) | copy-start | bytes 12582916
  61.2 0.8 %copy-start.3 = (f32[32,16,256]{2,1,0:T(8,128)}, f32[32,16,256]{2,1,0:T(8,128)S(1)}, u32[]{:S(2)}) copy-start(f32[32,16,256]{2,1,0:T(8,128)S(1)} %get-tuple-element.13.mas_ref) | copy-start | bytes 1572868
  62.0 0.8 %copy-start.4 = (f32[32,16,256]{2,1,0:T(8,128)}, f32[32,16,256]{2,1,0:T(8,128)S(1)}, u32[]{:S(2)}) copy-start(f32[32,16,256]{2,1,0:T(8,128)S(1)} %get-tuple-element.14.fir_ref) | copy-start | bytes 1572868
  62.8 0.8 %copy-start.5 = (f32[32,16,256]{2,1,0:T(8,128)}, f32[32,16,256]{2,1,0:T(8,128)S(1)}, u32[]{:S(2)}) copy-start(f32[32,16,256]{2,1,0:T(8,128)S(1)} %get-tuple-element.15.sec_ref) | copy-start | bytes 1572868

commit v2 on v0

v2 whole, which is shorter than its diff:
```python
import jax
import jax.numpy as jnp
from jax import lax
from jax.experimental import pallas as pl
from jax.experimental.pallas import tpu as pltpu
from jax.sharding import PartitionSpec as P

beta_one = 0.9
beta_two = 0.95
learning_rate = 0.003
decay_rate = 0.1
epsilon_value = 1e-08
adam_step = 100

MESH = pl.DeviceIdType.MESH
BF16 = jnp.bfloat16
F32 = jnp.float32

NZ = 8
NS = 32
CHIPS = 16
OWNERS = 28
SLOT_ROWS = 16
C = 256
SUBS = 4
R = C // SUBS
H = R // 2
CROSS = ((1, 0), (-1, 0), (0, 1), (0, -1), (2, 0), (0, 2))
ONWARD = (
    ((0, 1),),
    ((0, -1),),
    ((-1, 0),),
    ((1, 0),),
    ((0, 1), (0, -1)),
    ((1, 0), (-1, 0)),
)


def adam_update(master, adamw_first_moment, second_moment, gradient):
    corr_one = 1.0 - beta_one**adam_step
    corr_two = 1.0 - beta_two**adam_step
    first_new = beta_one * adamw_first_moment + (1.0 - beta_one) * gradient
    second_new = beta_two * second_moment + (1.0 - beta_two) * gradient * gradient
    direction = first_new / corr_one / (jnp.sqrt(second_new / corr_two) + epsilon_value)
    updated_master_weight = master - learning_rate * (direction + decay_rate * master)
    return (updated_master_weight, first_new, second_new)


def exchange_kernel(
    act_hbm, cot_hbm, mas_hbm, fir_hbm, sec_hbm, own_hbm,
    w_out, mas_out, fir_out, sec_out,
    act, cot, mas, fir, sec, own, load_sem,
    pick, st_send, st_land, st_cross, g_send, g_land, g_cross,
    far_send, far_recv, mid_send, mid_recv, near_send, near_recv, two_send, two_recv,
    keep, grad, own_w, new_mas, new_fir, new_sec,
    rs_send_sem, first_sem, last_sem, ag_send_sem, cross_sem, rest_sem, swap_send_sem, swap_sem,
    own_sem, move_send_sem, move_sem, move_swap_send_sem, move_swap_sem, out_sem,
):
    z = lax.axis_index("dp")
    me = lax.axis_index("shard")
    core = lax.rem(me, 2)
    chip = lax.div(me, 2)
    y = lax.rem(chip, 4)
    x = lax.div(chip, 4)

    def at_z(step):
        return lax.rem(z + step + NZ, NZ)

    def plane(dx, dy):
        return lax.rem(x + dx + 4, 4) * 4 + lax.rem(y + dy + 4, 4)

    def on_core(chip_id):
        return (z, chip_id * 2 + core)

    sibling = (z, chip * 2 + (1 - core))

    def remote(src, dst, send_sem, recv_sem, device):
        return pltpu.make_async_remote_copy(
            src_ref=src, dst_ref=dst, send_sem=send_sem, recv_sem=recv_sem,
            device_id=device, device_id_type=MESH,
        )

    def await_sent(ref, sem):
        remote(ref, ref, sem, sem, sibling).wait_send()

    def await_arrival(ref, sem):
        remote(ref, ref, sem, sem, sibling).wait_recv()

    def cot_load(r):
        start = pl.multiple_of(at_z(r) * C, C)
        return pltpu.make_async_copy(cot_hbm.at[:, pl.ds(start, C)], cot.at[r], load_sem.at[r])

    act_load = pltpu.make_async_copy(act_hbm, act, load_sem.at[8])
    state_loads = [
        pltpu.make_async_copy(own_hbm, own, load_sem.at[9]),
        pltpu.make_async_copy(mas_hbm, mas, load_sem.at[10]),
        pltpu.make_async_copy(fir_hbm, fir, load_sem.at[11]),
        pltpu.make_async_copy(sec_hbm, sec, load_sem.at[12]),
    ]
    act_load.start()
    for r in (4, 3, 5):
        cot_load(r).start()

    barrier = pltpu.get_barrier_semaphore()
    for step in (1, -1, 2, -2):
        pl.semaphore_signal(barrier, inc=1, device_id=(at_z(step), me), device_id_type=MESH)
    pl.semaphore_signal(barrier, inc=1, device_id=sibling, device_id_type=MESH)

    @pl.loop(1, CHIPS)
    def _(i):
        pl.semaphore_signal(
            barrier, inc=1, device_id=on_core(lax.rem(chip + i, CHIPS)), device_id_type=MESH
        )

    def partial(r):
        return lax.dot_general(
            cot[r], act[...], (((0,), (0,)), ((), ())), preferred_element_type=F32
        )

    act_load.wait()
    cot_load(4).wait()
    far_send[...] = partial(4).astype(BF16)
    cot_load(3).wait()
    cot_load(5).wait()
    for load in state_loads:
        load.start()
    for r in (2, 6, 1, 7, 0):
        cot_load(r).start()
    mid_send[0] = partial(3).astype(BF16)
    mid_send[1] = partial(5).astype(BF16)

    pl.semaphore_wait(barrier, 5 + CHIPS - 1)

    def rows_of(sub):
        return pl.ds(sub * R, R)

    def far_rows(sub, way):
        return pl.ds(sub * R + way * H, H)

    for sub in range(SUBS):
        for way in (0, 1):
            remote(
                far_send.at[far_rows(sub, way)], far_recv.at[way, pl.ds(sub * H, H)],
                rs_send_sem.at[0], first_sem.at[sub], (at_z(2 - 4 * way), me),
            ).start()
            remote(
                mid_send.at[way, rows_of(sub)], mid_recv.at[way, rows_of(sub)],
                rs_send_sem.at[0], first_sem.at[sub], (at_z(1 - 2 * way), me),
            ).start()

    for load in state_loads:
        load.wait()
    owner = own[...].astype(F32)
    row_id = lax.broadcasted_iota(jnp.int32, (NS, NS), 0)
    col_id = lax.broadcasted_iota(jnp.int32, (NS, NS), 1)
    wide = jnp.broadcast_to(owner, (NS, NS))
    tall = jnp.sum(jnp.where(row_id == col_id, wide, 0.0), axis=1, keepdims=True)
    rank = jnp.sum(jnp.where((wide == tall) & (row_id < col_id), 1.0, 0.0), axis=0, keepdims=True)
    key = jnp.broadcast_to(owner * 2.0 + rank, (16, NS)).astype(BF16)
    spread = lax.broadcasted_iota(jnp.int32, (NS, C), 0) == lax.div(
        lax.broadcasted_iota(jnp.int32, (NS, C), 1), 8
    )
    slot_of = jnp.dot(key, spread.astype(F32).astype(BF16), preferred_element_type=F32)[0:1]
    within = lax.rem(lax.broadcasted_iota(jnp.int32, (1, C), 1), 8).astype(F32)
    target_row = slot_of * 8.0 + within
    slot_row = lax.broadcasted_iota(jnp.int32, (OWNERS * SLOT_ROWS, C), 0).astype(F32)
    pick[...] = jnp.where(slot_row == target_row, 1.0, 0.0).astype(BF16)

    def packed(values):
        return (
            jnp.dot(pick[...], values, preferred_element_type=F32)
            .astype(BF16)
            .reshape(OWNERS // 2, 2, SLOT_ROWS, C)
        )

    st_send[:, :, 0] = packed(mas[...].astype(BF16))
    st_send[:, :, 1] = packed(fir[...].astype(BF16))
    st_send[:, :, 2] = packed(sec[...].astype(BF16))

    def move_out(send, land, index):
        @pl.loop(1, CHIPS)
        def _(i):
            to = lax.rem(chip + i, CHIPS)

            @pl.when(to < OWNERS // 2)
            def _():
                remote(
                    send.at[to], land.at[chip], move_send_sem.at[index], move_sem.at[index],
                    on_core(to),
                ).start()

        @pl.when(chip < OWNERS // 2)
        def _():
            land[chip] = send[chip]

    def move_across(land, cross, index):
        @pl.when(chip < OWNERS // 2)
        def _():
            await_arrival(land.at[pl.ds(0, CHIPS - 1)], move_sem.at[index])
            remote(
                land.at[:, 1 - core], cross, move_swap_send_sem.at[index], move_swap_sem.at[index],
                sibling,
            ).start()

    def move_sent(send, index):
        @pl.when(chip < OWNERS // 2)
        def _():
            await_sent(send.at[pl.ds(0, OWNERS // 2 - 1)], move_send_sem.at[index])

        @pl.when(chip >= OWNERS // 2)
        def _():
            await_sent(send, move_send_sem.at[index])

    move_out(st_send, st_land, 0)

    for r in (2, 6):
        cot_load(r).wait()
    keep[1] = partial(2)
    keep[2] = partial(6)
    for r in (1, 7):
        cot_load(r).wait()
    near_send[0] = partial(1).astype(BF16)
    near_send[1] = partial(7).astype(BF16)

    for sub in range(SUBS):
        await_arrival(w_out.at[pl.ds(0, 3), 0, rows_of(sub)], first_sem.at[sub])
        for way in (0, 1):
            both = pl.ds(sub * R + way * H, H)
            single = pl.ds(sub * R + (1 - way) * H, H)
            two_send[way, both] = (
                keep[1 + way, both]
                + mid_recv[way, both].astype(F32)
                + far_recv[way, pl.ds(sub * H, H)].astype(F32)
            ).astype(BF16)
            two_send[way, single] = (
                keep[1 + way, single] + mid_recv[way, single].astype(F32)
            ).astype(BF16)
            remote(
                two_send.at[way, rows_of(sub)], two_recv.at[way, rows_of(sub)],
                rs_send_sem.at[0], last_sem.at[sub], (at_z(2 - 4 * way), me),
            ).start()
        for way in (0, 1):
            remote(
                near_send.at[way, rows_of(sub)], near_recv.at[way, rows_of(sub)],
                rs_send_sem.at[0], last_sem.at[sub], (at_z(1 - 2 * way), me),
            ).start()

    cot_load(0).wait()
    keep[0] = partial(0)

    def gather_send(sub, src, source, to, sem, first=0, count=R):
        dst = w_out.at[source, core, pl.ds(sub * R + first, count)]
        remote(dst if src is None else src, dst, ag_send_sem.at[sub], sem, on_core(to)).start()

    def update(sub):
        rows = rows_of(sub)
        await_arrival(w_out.at[pl.ds(0, 4), 0, rows], last_sem.at[sub])
        total = keep[0, rows]
        for way in (0, 1):
            total = total + near_recv[way, rows].astype(F32) + two_recv[way, rows].astype(F32)
        new_master, _, _ = adam_update(mas[rows], fir[rows], sec[rows], total)
        own_w[rows] = new_master.astype(BF16)
        for index, (dx, dy) in enumerate(CROSS):
            gather_send(sub, own_w.at[rows], chip, plane(dx, dy), cross_sem.at[sub, index])
        pltpu.make_async_copy(own_w.at[rows], w_out.at[chip, core, rows], own_sem.at[sub]).start()
        grad[rows] = total.astype(BF16)

    def forward(sub):
        for index, (dx, dy) in enumerate(CROSS):
            source = plane(-dx, -dy)
            await_arrival(w_out.at[source, core, rows_of(sub)], cross_sem.at[sub, index])
            for tx, ty in ONWARD[index]:
                gather_send(sub, None, source, plane(tx, ty), rest_sem.at[sub])
        gather_send(sub, None, plane(2, 0), plane(0, 2), rest_sem.at[sub], 0, H)
        gather_send(sub, None, plane(0, 2), plane(2, 0), rest_sem.at[sub], H, H)

    def swap(sub):
        rows = rows_of(sub)
        await_arrival(w_out.at[pl.ds(0, 9), 0, rows], rest_sem.at[sub])
        pltpu.make_async_copy(own_w.at[rows], w_out.at[chip, core, rows], own_sem.at[sub]).wait()
        half = w_out.at[:, core, rows]
        remote(half, half, swap_send_sem.at[sub], swap_sem.at[sub], sibling).start()

    def settle(sub):
        await_arrival(w_out.at[:, 1 - core, rows_of(sub)], swap_sem.at[sub])
        await_sent(w_out.at[:, core, rows_of(sub)], swap_send_sem.at[sub])
        await_sent(w_out.at[pl.ds(0, 15), 0, rows_of(sub)], ag_send_sem.at[sub])

    def send_gradient():
        g_send[...] = packed(grad[...])
        move_out(g_send, g_land, 1)

    def own_blocks():
        @pl.when(chip < OWNERS // 2)
        def _():
            for cross, index in ((st_cross, 0), (g_cross, 1)):
                await_arrival(cross, move_swap_sem.at[index])

            @pl.loop(0, CHIPS)
            def _(source):
                for state, gradient, slot in (
                    (st_land.at[source, core], g_land.at[source, core], source * 2 + core),
                    (st_cross.at[source], g_cross.at[source], source * 2 + (1 - core)),
                ):
                    updated = adam_update(
                        state[0].astype(F32), state[1].astype(F32), state[2].astype(F32),
                        gradient[...].astype(F32),
                    )
                    new_mas[slot], new_fir[slot], new_sec[slot] = updated

        @pl.when(chip >= OWNERS // 2)
        def _():
            for new in (new_mas, new_fir, new_sec):
                new[...] = jnp.zeros_like(new)

        for index, (new, out) in enumerate(out_pairs):
            pltpu.make_async_copy(new, out, out_sem.at[index]).start()

    out_pairs = ((new_mas, mas_out), (new_fir, fir_out), (new_sec, sec_out))

    update(0)
    update(1)
    move_across(st_land, st_cross, 0)
    forward(0)
    update(2)
    forward(1)
    update(3)
    send_gradient()
    forward(2)
    swap(0)
    forward(3)
    swap(1)
    move_across(g_land, g_cross, 1)
    swap(2)
    own_blocks()
    swap(3)
    settle(0)
    settle(1)
    settle(2)
    settle(3)

    await_sent(w_out.at[pl.ds(0, 7), 0], rs_send_sem.at[0])
    for index, (new, out) in enumerate(out_pairs):
        pltpu.make_async_copy(new, out, out_sem.at[index]).wait()
    for index, (send, land, cross) in enumerate(
        ((st_send, st_land, st_cross), (g_send, g_land, g_cross))
    ):
        move_sent(send, index)

        @pl.when(chip < OWNERS // 2)
        def _():
            await_sent(cross, move_swap_send_sem.at[index])


def store_kernel(w_ref, mas_ref, fir_ref, sec_ref, weights, out_mas, out_fir, out_sec, sem):
    copies = [
        pltpu.make_async_copy(
            w_ref.at[s // 2, s % 2], weights.at[:, pl.ds(s * C, C)], sem.at[s]
        )
        for s in range(NS)
    ]
    copies.append(pltpu.make_async_copy(mas_ref, out_mas, sem.at[NS]))
    copies.append(pltpu.make_async_copy(fir_ref, out_fir, sem.at[NS + 1]))
    copies.append(pltpu.make_async_copy(sec_ref, out_sec, sem.at[NS + 2]))
    for copy in copies:
        copy.start()
    for copy in copies:
        copy.wait()


def shards(activations, cotangent, master, adamw_first_moment, second_moment, new_owner):
    tokens = activations.shape[0]
    moved = (NS, SLOT_ROWS, C)
    anywhere = pl.BlockSpec(memory_space=pl.ANY)
    vmem = pl.BlockSpec(memory_space=pltpu.VMEM)
    dma = pltpu.SemaphoreType.DMA
    gathered, mas, fir, sec = pl.pallas_call(
        exchange_kernel,
        out_shape=(
            pltpu.VMEM((CHIPS, 2, C, C), BF16),
            pltpu.VMEM(moved, F32),
            pltpu.VMEM(moved, F32),
            pltpu.VMEM(moved, F32),
        ),
        in_specs=[anywhere] * 6,
        out_specs=[anywhere] * 4,
        scratch_shapes=[
            pltpu.VMEM((tokens, C), BF16),
            pltpu.VMEM((NZ, tokens, C), BF16),
            pltpu.VMEM((C, C), F32),
            pltpu.VMEM((C, C), F32),
            pltpu.VMEM((C, C), F32),
            pltpu.VMEM((1, NS), jnp.int32),
            dma((13,)),
            pltpu.VMEM((OWNERS * SLOT_ROWS, C), BF16),
            pltpu.VMEM((OWNERS // 2, 2, 3, SLOT_ROWS, C), BF16),
            pltpu.VMEM((CHIPS, 2, 3, SLOT_ROWS, C), BF16),
            pltpu.VMEM((CHIPS, 3, SLOT_ROWS, C), BF16),
            pltpu.VMEM((OWNERS // 2, 2, SLOT_ROWS, C), BF16),
            pltpu.VMEM((CHIPS, 2, SLOT_ROWS, C), BF16),
            pltpu.VMEM((CHIPS, SLOT_ROWS, C), BF16),
            pltpu.VMEM((C, C), BF16),
            pltpu.VMEM((2, C // 2, C), BF16),
            pltpu.VMEM((2, C, C), BF16),
            pltpu.VMEM((2, C, C), BF16),
            pltpu.VMEM((2, C, C), BF16),
            pltpu.VMEM((2, C, C), BF16),
            pltpu.VMEM((2, C, C), BF16),
            pltpu.VMEM((2, C, C), BF16),
            pltpu.VMEM((3, C, C), F32),
            pltpu.VMEM((C, C), BF16),
            pltpu.VMEM((C, C), BF16),
            pltpu.VMEM(moved, F32),
            pltpu.VMEM(moved, F32),
            pltpu.VMEM(moved, F32),
            dma((1,)),
            dma((SUBS,)),
            dma((SUBS,)),
            dma((SUBS,)),
            dma((SUBS, len(CROSS))),
            dma((SUBS,)),
            dma((SUBS,)),
            dma((SUBS,)),
            dma((SUBS,)),
            dma((2,)),
            dma((2,)),
            dma((2,)),
            dma((2,)),
            dma((3,)),
        ],
        compiler_params=pltpu.CompilerParams(
            collective_id=0, has_side_effects=True, vmem_limit_bytes=40 * 2**20
        ),
        name="exchange",
    )(
        *[
            pltpu.with_memory_space_constraint(operand, pltpu.HBM)
            for operand in (
                activations, cotangent, master, adamw_first_moment, second_moment,
                new_owner.reshape(1, NS),
            )
        ]
    )
    weights, mas, fir, sec = pl.pallas_call(
        store_kernel,
        out_shape=(
            jax.ShapeDtypeStruct((C, NS * C), BF16),
            jax.ShapeDtypeStruct(moved, F32),
            jax.ShapeDtypeStruct(moved, F32),
            jax.ShapeDtypeStruct(moved, F32),
        ),
        in_specs=[vmem] * 4,
        out_specs=[anywhere] * 4,
        scratch_shapes=[dma((NS + 3,))],
        compiler_params=pltpu.CompilerParams(vmem_limit_bytes=8 * 2**20),
        name="store",
    )(
        *[
            pltpu.with_memory_space_constraint(operand, pltpu.VMEM)
            for operand in (gathered, mas, fir, sec)
        ]
    )
    out_shape = (1, 1, NS, 2, SLOT_ROWS // 2, C)
    return (weights, mas.reshape(out_shape), fir.reshape(out_shape), sec.reshape(out_shape))


def solution(mesh):
    in_specs = (
        P("dp", "shard"),
        P("dp", None),
        P("dp", "shard"),
        P("dp", "shard"),
        P("dp", "shard"),
        P("dp", "shard", None),
    )
    out_specs = (
        P("dp", None),
        P("dp", "shard", None, None, None, None),
        P("dp", "shard", None, None, None, None),
        P("dp", "shard", None, None, None, None),
    )
    return jax.shard_map(shards, mesh=mesh, in_specs=in_specs, out_specs=out_specs, check_vma=False)
```

time: 132 us -> 46.4 us (0.35)
  waiting for transfers between devices: 78.4 us -> 0 us
  Pallas kernels: 0 us -> 45.7 us
  starting transfers between devices: 19.9 us -> 0 us
  between operations: 14.2 us -> 0.64 us
  local copies, waits for them, and re-layouts: 11.4 us -> 0 us
  matrix products: 5.56 us -> 0 us
  other arithmetic: 1.97 us -> 0 us
    pallas_call x0 -> x2, Pallas kernels: none -> 45.7 us  [the longest x1 42.9 us: shards(): pl.pallas_call(exchange_kernel, out_shape=(pltpu.VMEM((CHIPS, 2, C, C), B...]
    reduce_scatter x1 -> x0, waiting for transfers between devices: 37.6 us -> none  [shards(): lax.psum_scatter(lax.dot_general(cotangent, activations, (((0,), (0,)), (...]
    all_to_all x3 -> x0, waiting for transfers between devices: 35 us -> none  [the longest x1 14.2 us: shards(): lax.all_to_all(pack_slots(second_new), 'shard', split_axis=0, concat_axis...]
    all_to_all x3 -> x0, starting transfers between devices: 19.8 us -> none  [the longest x1 12.5 us: shards(): lax.all_to_all(pack_slots(updated_master_weight), 'shard', split_axis=0,...]
    unnamed x14 -> x0, local copies, waits for them, and re-layouts: 7.99 us -> none
    all_gather x1 -> x0, waiting for transfers between devices: 5.68 us -> none  [shards(): lax.all_gather(updated_master_weight.astype(jnp.bfloat16), 'shard', axis=...]
    dot_general x4 -> x0, matrix products: 5.56 us -> none  [the longest x1 4.49 us: shards(): lax.dot_general(cotangent, activations, (((0,), (0,)), ((), ())), preferr...]
    dot_general x3 -> x0, local copies, waits for them, and re-layouts: 3.3 us -> none  [pack_slots(): jnp.einsum('trk,kx->trx', selector, blocks, precision=lax.Precision.HIGHEST)]
  transfers between devices with their start and end apart: 5 -> 0, of which waited for: 5 -> 0; matrix products, arithmetic and copies ran while one was open for 4% -> 0% of each run, Pallas kernels for 0% -> 0%
where the time goes in v2:
time: 46.4 us; the launch traced here: 46.3 us
  Pallas kernels  45.7 us (98%)
  between operations  0.64 us (1%)
    pallas_call x1, Pallas kernels, shards(): pl.pallas_call(exchange_kernel, out_shape=(pltpu.VMEM((CHIPS, 2, C, C), B...  42.9 us
    pallas_call x1, Pallas kernels, shards(): pl.pallas_call(store_kernel, out_shape=(jax.ShapeDtypeStruct((C, NS * C),...  2.79 us

profile of v2, /device:TPU:1, one launch (start us, length us, event | category | flops | bytes accessed | tf_op | source)
XLA Modules:
  0.0 46.3 jit_solution(6812923985608593697)
XLA Ops:
  0.6 42.9 %exchange.1 = (bf16[16,2,256,256]{3,2,1,0:T(8,128)(2,1)S(1)}, f32[32,16,256]{2,1,0:T(8,128)S(1)}, f32[32,16,256]{2,1,0:T(8,128)S(1)}, f32[32,16,256]{2,1,0:T(8,128)S(1)}) custom-call(bf16[1024,256]{1,0:T(8,128)(2,1)} %act_hbm.1, bf16[1024,2048]{1,0:T(8,128)(2,1)} %cot_hbm.1, f32[256,256]{1,0:T(8,128)} %mas_hbm.1, f32[256,256]{1,0:T(8,128)} %fir_hbm.1, ...), custom_call_target="tpu_custom_call" | custom-call | tf_op jit(solution)/shard_map/exchange/pallas_call | solution.py:377
  43.5 2.8 %store.1 = (bf16[256,8192]{1,0:T(8,128)(2,1)}, f32[32,16,256]{2,1,0:T(8,128)}, f32[32,16,256]{2,1,0:T(8,128)}, f32[32,16,256]{2,1,0:T(8,128)}) custom-call(bf16[16,2,256,256]{3,2,1,0:T(8,128)(2,1)S(1)} %get-tuple-element.12.w_ref, f32[32,16,256]{2,1,0:T(8,128)S(1)} %get-tuple-element.13.mas_ref, f32[32,16,256]{2,1,0:T(8,128)S(1)} %get-tuple-element.14.fir_ref, ...), custom_call_target="tpu_custom_call" | custom-call | tf_op jit(solution)/shard_map/store/pallas_call | solution.py:444

commit v3 on v2

v3 whole, which is shorter than its diff:
```python
import jax
import jax.numpy as jnp
from jax import lax
from jax.experimental import pallas as pl
from jax.experimental.pallas import tpu as pltpu
from jax.sharding import PartitionSpec as P

beta_one = 0.9
beta_two = 0.95
learning_rate = 0.003
decay_rate = 0.1
epsilon_value = 1e-08
adam_step = 100

MESH = pl.DeviceIdType.MESH
BF16 = jnp.bfloat16
F32 = jnp.float32

NZ = 8
NS = 32
CHIPS = 16
OWNERS = 28
SLOT_ROWS = 16
C = 256
ROWS = (64, 64, 64, 64)
SUBS = len(ROWS)
START = tuple(sum(ROWS[:sub]) for sub in range(SUBS))
DIRECT = 4
CROSS = ((1, 0), (-1, 0), (0, 1), (0, -1), (2, 0), (0, 2))
ONWARD = (
    ((0, 1),),
    ((0, -1),),
    ((-1, 0),),
    ((1, 0),),
    ((0, 1), (0, -1)),
    ((1, 0), (-1, 0)),
)
FIRST_REST = (0, 1, 2, 3, 4, 6)


def moments(adamw_first_moment, second_moment, gradient):
    first_new = beta_one * adamw_first_moment + (1.0 - beta_one) * gradient
    second_new = beta_two * second_moment + (1.0 - beta_two) * gradient * gradient
    return first_new, second_new


def adam_update(master, adamw_first_moment, second_moment, gradient):
    corr_one = 1.0 - beta_one**adam_step
    corr_two = 1.0 - beta_two**adam_step
    first_new, second_new = moments(adamw_first_moment, second_moment, gradient)
    direction = first_new / corr_one / (jnp.sqrt(second_new / corr_two) + epsilon_value)
    return master - learning_rate * (direction + decay_rate * master)


def exchange_kernel(
    act_hbm, cot_hbm, mas_hbm, fir_hbm, sec_hbm, own_hbm,
    w_out, where_out, fir_out, sec_out,
    act, cot, mas, fir, sec, own, load_sem,
    own_line, own_land, own_cross, place, pick, st_send, st_land, st_cross, g_send, g_land, g_cross,
    far_send, far_recv, mid_send, mid_recv, near_send, near_recv, two_send, two_recv,
    keep, grad, own_w, new_fir, new_sec,
    rs_send_sem, first_sem, second_sem, last_sem, ag_send_sem, cross_sem, rest_sem, last_rest_sem, swap_send_sem, swap_sem,
    own_sem, move_send_sem, move_sem, move_swap_send_sem, move_swap_sem, out_sem,
):
    z = lax.axis_index("dp")
    me = lax.axis_index("shard")
    core = lax.rem(me, 2)
    chip = lax.div(me, 2)
    y = lax.rem(chip, 4)
    x = lax.div(chip, 4)

    def at_z(step):
        return lax.rem(z + step + NZ, NZ)

    def plane(dx, dy):
        return lax.rem(x + dx + 4, 4) * 4 + lax.rem(y + dy + 4, 4)

    def on_core(chip_id):
        return (z, chip_id * 2 + core)

    sibling = (z, chip * 2 + (1 - core))

    def remote(src, dst, send_sem, recv_sem, device):
        return pltpu.make_async_remote_copy(
            src_ref=src, dst_ref=dst, send_sem=send_sem, recv_sem=recv_sem,
            device_id=device, device_id_type=MESH,
        )

    def await_sent(ref, sem):
        remote(ref, ref, sem, sem, sibling).wait_send()

    def await_arrival(ref, sem):
        remote(ref, ref, sem, sem, sibling).wait_recv()

    def cot_load(r):
        start = pl.multiple_of(at_z(r) * C, C)
        return pltpu.make_async_copy(cot_hbm.at[:, pl.ds(start, C)], cot.at[r], load_sem.at[r])

    act_load = pltpu.make_async_copy(act_hbm, act, load_sem.at[8])
    state_loads = [
        pltpu.make_async_copy(own_hbm, own, load_sem.at[9]),
        pltpu.make_async_copy(mas_hbm, mas, load_sem.at[10]),
        pltpu.make_async_copy(fir_hbm, fir, load_sem.at[11]),
        pltpu.make_async_copy(sec_hbm, sec, load_sem.at[12]),
    ]
    act_load.start()
    for r in (4, 3, 5):
        cot_load(r).start()

    barrier = pltpu.get_barrier_semaphore()
    for step in (1, -1, 2, -2):
        pl.semaphore_signal(barrier, inc=1, device_id=(at_z(step), me), device_id_type=MESH)
    pl.semaphore_signal(barrier, inc=1, device_id=sibling, device_id_type=MESH)

    @pl.loop(1, CHIPS)
    def _(i):
        pl.semaphore_signal(
            barrier, inc=1, device_id=on_core(lax.rem(chip + i, CHIPS)), device_id_type=MESH
        )

    def partial(r):
        return lax.dot_general(
            cot[r], act[...], (((0,), (0,)), ((), ())), preferred_element_type=F32
        )

    act_load.wait()
    cot_load(4).wait()
    far_send[...] = partial(4).astype(BF16)
    cot_load(3).wait()
    cot_load(5).wait()
    for load in state_loads:
        load.start()
    for r in (2, 6, 1, 7, 0):
        cot_load(r).start()
    mid_send[0] = partial(3).astype(BF16)
    mid_send[1] = partial(5).astype(BF16)

    pl.semaphore_wait(barrier, 5 + CHIPS - 1)

    def rows_of(sub):
        return pl.ds(START[sub], ROWS[sub])

    def half_of(sub, way):
        return pl.ds(START[sub] + way * (ROWS[sub] // 2), ROWS[sub] // 2)

    def far_slot(sub):
        return pl.ds(START[sub] // 2, ROWS[sub] // 2)

    def reduce_first(sub):
        for way in (0, 1):
            remote(
                far_send.at[half_of(sub, way)], far_recv.at[way, far_slot(sub)],
                rs_send_sem.at[0], first_sem.at[sub], (at_z(2 - 4 * way), me),
            ).start()
            remote(
                mid_send.at[way, rows_of(sub)], mid_recv.at[way, rows_of(sub)],
                rs_send_sem.at[0], first_sem.at[sub], (at_z(1 - 2 * way), me),
            ).start()

    def multiply_two():
        for r in (2, 6):
            cot_load(r).wait()
        keep[1] = partial(2)
        keep[2] = partial(6)

    def multiply_one():
        for r in (1, 7):
            cot_load(r).wait()
        keep[3] = partial(1)
        keep[4] = partial(7)

    def multiply_own():
        cot_load(0).wait()
        keep[0] = partial(0)

    def send_near(sub, way):
        remote(
            near_send.at[way, rows_of(sub)], near_recv.at[way, rows_of(sub)],
            rs_send_sem.at[0], last_sem.at[sub], (at_z(1 - 2 * way), me),
        ).start()

    def reduce_second(sub):
        rows = rows_of(sub)
        direct = sub < DIRECT
        await_arrival(w_out.at[pl.ds(0, 3), 0, rows], first_sem.at[sub])
        for way in (0, 1):
            both = half_of(sub, way)
            single = half_of(sub, 1 - way)
            two_send[way, both] = (
                keep[1 + way, both]
                + mid_recv[way, both].astype(F32)
                + far_recv[way, far_slot(sub)].astype(F32)
            ).astype(BF16)
            two_send[way, single] = (
                keep[1 + way, single] + mid_recv[way, single].astype(F32)
            ).astype(BF16)
            remote(
                two_send.at[way, rows], two_recv.at[way, rows], rs_send_sem.at[0],
                last_sem.at[sub] if direct else second_sem.at[sub],
                (at_z((1 + direct) * (1 - 2 * way)), me),
            ).start()
        if direct:
            for way in (0, 1):
                near_send[way, rows] = keep[3 + way, rows].astype(BF16)
                send_near(sub, way)

    def reduce_third(sub):
        rows = rows_of(sub)
        await_arrival(w_out.at[pl.ds(0, 2), 0, rows], second_sem.at[sub])
        for way in (0, 1):
            near_send[way, rows] = (
                keep[3 + way, rows] + two_recv[way, rows].astype(F32)
            ).astype(BF16)
            send_near(sub, way)

    def packed(values):
        return (
            jnp.dot(pick[...], values, preferred_element_type=F32)
            .astype(BF16)
            .reshape(OWNERS // 2, 2, SLOT_ROWS, C)
        )

    def pack_state():
        for load in state_loads:
            load.wait()
        own_line[...] = jnp.full_like(own_line, -1)
        own_line[:, 0:NS] = own[...]
        move_out(own_line, own_land, 2, lambda to: own_line)
        owner = own[...].astype(F32)
        row_id = lax.broadcasted_iota(jnp.int32, (NS, NS), 0)
        col_id = lax.broadcasted_iota(jnp.int32, (NS, NS), 1)
        wide = jnp.broadcast_to(owner, (NS, NS))
        tall = jnp.sum(jnp.where(row_id == col_id, wide, 0.0), axis=1, keepdims=True)
        rank = jnp.sum(jnp.where((wide == tall) & (row_id < col_id), 1.0, 0.0), axis=0, keepdims=True)
        key = jnp.broadcast_to(owner * 2.0 + rank, (16, NS)).astype(BF16)
        spread = lax.broadcasted_iota(jnp.int32, (NS, C), 0) == lax.div(
            lax.broadcasted_iota(jnp.int32, (NS, C), 1), 8
        )
        slot_of = jnp.dot(key, spread.astype(F32).astype(BF16), preferred_element_type=F32)[0:1]
        within = lax.rem(lax.broadcasted_iota(jnp.int32, (1, C), 1), 8).astype(F32)
        target_row = slot_of * 8.0 + within
        slot_row = lax.broadcasted_iota(jnp.int32, (OWNERS * SLOT_ROWS, C), 0).astype(F32)
        pick[...] = jnp.where(slot_row == target_row, 1.0, 0.0).astype(BF16)

        st_send[:, :, 0] = packed(fir[...].astype(BF16))
        st_send[:, :, 1] = packed(sec[...].astype(BF16))
        move_out(st_send, st_land, 0)

    def move_out(send, land, index, piece=None):
        if piece is None:
            piece = lambda to: send.at[to]

        @pl.loop(1, CHIPS)
        def _(i):
            to = lax.rem(chip + i, CHIPS)

            @pl.when(to < OWNERS // 2)
            def _():
                remote(
                    piece(to), land.at[chip], move_send_sem.at[index], move_sem.at[index],
                    on_core(to),
                ).start()

        @pl.when(chip < OWNERS // 2)
        def _():
            land[chip] = piece(chip)[...]

    def move_across(land, cross, index):
        @pl.when(chip < OWNERS // 2)
        def _():
            await_arrival(land.at[pl.ds(0, CHIPS - 1)], move_sem.at[index])
            remote(
                land if index == 2 else land.at[:, 1 - core], cross,
                move_swap_send_sem.at[index], move_swap_sem.at[index], sibling,
            ).start()

    def move_sent(land, index):
        @pl.when(chip < OWNERS // 2)
        def _():
            await_sent(land.at[pl.ds(0, OWNERS // 2 - 1)], move_send_sem.at[index])

        @pl.when(chip >= OWNERS // 2)
        def _():
            await_sent(land.at[pl.ds(0, OWNERS // 2)], move_send_sem.at[index])

    def gather_send(sub, src, source, to, sem, rows=None):
        dst = w_out.at[source, core, rows_of(sub) if rows is None else rows]
        remote(dst if src is None else src, dst, ag_send_sem.at[sub], sem, on_core(to)).start()

    def update(sub):
        rows = rows_of(sub)
        direct = sub < DIRECT
        await_arrival(w_out.at[pl.ds(0, 2 + 2 * direct), 0, rows], last_sem.at[sub])
        total = keep[0, rows]
        for way in (0, 1):
            total = total + near_recv[way, rows].astype(F32)
            if direct:
                total = total + two_recv[way, rows].astype(F32)
        new_master = adam_update(mas[rows], fir[rows], sec[rows], total)
        own_w[rows] = new_master.astype(BF16)
        for index, (dx, dy) in enumerate(CROSS):
            gather_send(sub, own_w.at[rows], chip, plane(dx, dy), cross_sem.at[sub, index])
        pltpu.make_async_copy(own_w.at[rows], w_out.at[chip, core, rows], own_sem.at[sub]).start()
        if sub == SUBS - 1:
            swap_one(chip, own_w.at[rows])
        grad[rows] = total.astype(BF16)

    def forward(sub):
        for index, (dx, dy) in enumerate(CROSS):
            source = plane(-dx, -dy)
            await_arrival(w_out.at[source, core, rows_of(sub)], cross_sem.at[sub, index])
            for order, (tx, ty) in enumerate(ONWARD[index]):
                gather_send(
                    sub, None, source, plane(tx, ty), rest_arrival(sub, FIRST_REST[index] + order)
                )
            if index >= 4:
                gather_send(
                    sub, None, source, plane(dy, dx), rest_arrival(sub, 8), half_of(sub, index - 4)
                )
            if sub == SUBS - 1:
                swap_one(source)

    def rest_arrival(sub, order):
        return last_rest_sem.at[order] if sub == SUBS - 1 else rest_sem.at[sub]

    def swap_one(source, src=None):
        sub = SUBS - 1
        dst = w_out.at[source, core, rows_of(sub)]
        remote(
            dst if src is None else src, dst, swap_send_sem.at[sub], swap_sem.at[sub], sibling
        ).start()

    def swap(sub):
        rows = rows_of(sub)
        if sub < SUBS - 1:
            await_arrival(w_out.at[pl.ds(0, 9), 0, rows], rest_sem.at[sub])
            pltpu.make_async_copy(own_w.at[rows], w_out.at[chip, core, rows], own_sem.at[sub]).wait()
            half = w_out.at[:, core, rows]
            remote(half, half, swap_send_sem.at[sub], swap_sem.at[sub], sibling).start()
            return
        for index, (dx, dy) in enumerate(CROSS):
            for order, (tx, ty) in enumerate(ONWARD[index]):
                source = plane(-dx - tx, -dy - ty)
                await_arrival(
                    w_out.at[source, core, rows], rest_arrival(sub, FIRST_REST[index] + order)
                )
                swap_one(source)
        source = plane(2, 2)
        await_arrival(w_out.at[source, core, rows], rest_arrival(sub, 8))
        swap_one(source)
        pltpu.make_async_copy(own_w.at[rows], w_out.at[chip, core, rows], own_sem.at[sub]).wait()

    def settle(sub):
        await_arrival(w_out.at[:, 1 - core, rows_of(sub)], swap_sem.at[sub])
        await_sent(w_out.at[:, core, rows_of(sub)], swap_send_sem.at[sub])
        await_sent(w_out.at[pl.ds(0, 15), 0, rows_of(sub)], ag_send_sem.at[sub])

    def send_gradient():
        g_send[...] = packed(grad[...])
        move_out(g_send, g_land, 1)

    def find_places():
        place[...] = jnp.full_like(place, -1)

        @pl.when(chip < OWNERS // 2)
        def _():
            await_arrival(own_cross, move_swap_sem.at[2])
            lane = lax.broadcasted_iota(jnp.int32, (CHIPS, 128), 1)
            for index, owners in enumerate((own_land, own_cross)):
                mine = owners[...].reshape(CHIPS, 128) == me
                first = jnp.min(jnp.where(mine, lane, 128), axis=1, keepdims=True)
                last = jnp.max(jnp.where(mine, lane, -1), axis=1, keepdims=True)
                place[index] = jnp.where(
                    lane == 0,
                    jnp.where(first < 128, first, -1),
                    jnp.where((lane == 1) & (last > first), last, -1),
                )

        pltpu.make_async_copy(place, where_out, out_sem.at[2]).start()

    def own_blocks():
        @pl.when(chip < OWNERS // 2)
        def _():
            for cross, index in ((st_cross, 0), (g_cross, 1)):
                await_arrival(cross, move_swap_sem.at[index])

            @pl.loop(0, CHIPS)
            def _(source):
                for state, gradient, slot in (
                    (st_land.at[source, core], g_land.at[source, core], source * 2 + core),
                    (st_cross.at[source], g_cross.at[source], source * 2 + (1 - core)),
                ):
                    new_fir[slot], new_sec[slot] = moments(
                        state[0].astype(F32), state[1].astype(F32), gradient[...].astype(F32)
                    )

        @pl.when(chip >= OWNERS // 2)
        def _():
            for new in (new_fir, new_sec):
                new[...] = jnp.zeros_like(new)

        pltpu.make_async_copy(new_fir, fir_out, out_sem.at[0]).start()
        pltpu.make_async_copy(new_sec, sec_out, out_sem.at[1]).start()

    reduce_first(0)
    reduce_first(1)
    reduce_first(2)
    pack_state()
    multiply_two()
    multiply_one()
    reduce_second(0)
    reduce_first(3)
    multiply_own()
    reduce_second(1)
    reduce_second(2)
    update(0)
    reduce_second(3)
    update(1)
    forward(0)
    update(2)
    forward(1)
    update(3)
    pl.when(core == 0)(send_gradient)
    forward(2)
    move_across(own_land, own_cross, 2)
    move_across(st_land, st_cross, 0)
    swap(0)
    forward(3)
    pl.when(core == 1)(send_gradient)
    swap(1)
    move_across(g_land, g_cross, 1)
    swap(2)
    swap(3)
    find_places()
    own_blocks()
    settle(0)
    settle(1)
    settle(2)
    settle(3)

    await_sent(w_out.at[pl.ds(0, 7), 0], rs_send_sem.at[0])
    pltpu.make_async_copy(new_fir, fir_out, out_sem.at[0]).wait()
    pltpu.make_async_copy(new_sec, sec_out, out_sem.at[1]).wait()
    pltpu.make_async_copy(place, where_out, out_sem.at[2]).wait()
    for index, (land, cross) in enumerate(
        ((st_land, st_cross), (g_land, g_cross), (own_land, own_cross))
    ):
        move_sent(land, index)

        @pl.when(chip < OWNERS // 2)
        def _():
            await_sent(cross, move_swap_send_sem.at[index])


def store_kernel(
    w_ref, where_ref, fir_ref, sec_ref, weights, out_mas, out_fir, out_sec, new_mas, places, sem
):
    core = lax.rem(lax.axis_index("shard"), 2)
    where_copy = pltpu.make_async_copy(where_ref, places, sem.at[NS])
    where_copy.start()
    copies = [
        pltpu.make_async_copy(
            w_ref.at[s // 2, s % 2], weights.at[:, pl.ds(s * C, C)], sem.at[s]
        )
        for s in range(NS)
    ]
    copies.append(pltpu.make_async_copy(fir_ref, out_fir, sem.at[NS + 1]))
    copies.append(pltpu.make_async_copy(sec_ref, out_sec, sem.at[NS + 2]))
    for copy in copies:
        copy.start()

    where_copy.wait()

    @pl.loop(0, CHIPS)
    def _(source):
        for index in range(2):
            side = lax.rem(core + index, 2)
            for slot in range(2):
                block = places[index, source, slot]
                held = jnp.maximum(block, 0)
                start = pl.multiple_of(lax.div(held, 2) * 16, 16)
                tile = w_ref[source, side, pl.ds(start, 16)].astype(F32)
                rows = jnp.where(lax.rem(held, 2) == 1, tile[8:16], tile[0:8])
                new_mas[source * 2 + side, pl.ds(slot * 8, 8)] = jnp.where(block >= 0, rows, 0.0)

    copies.append(pltpu.make_async_copy(new_mas, out_mas, sem.at[NS + 3]))
    copies[-1].start()
    for copy in copies:
        copy.wait()


def shards(activations, cotangent, master, adamw_first_moment, second_moment, new_owner):
    tokens = activations.shape[0]
    moved = (NS, SLOT_ROWS, C)
    anywhere = pl.BlockSpec(memory_space=pl.ANY)
    vmem = pl.BlockSpec(memory_space=pltpu.VMEM)
    dma = pltpu.SemaphoreType.DMA
    gathered, where, fir, sec = pl.pallas_call(
        exchange_kernel,
        out_shape=(
            pltpu.VMEM((CHIPS, 2, C, C), BF16),
            pltpu.VMEM((2, CHIPS, 128), jnp.int32),
            pltpu.VMEM(moved, F32),
            pltpu.VMEM(moved, F32),
        ),
        in_specs=[anywhere] * 6,
        out_specs=[anywhere] * 4,
        scratch_shapes=[
            pltpu.VMEM((tokens, C), BF16),
            pltpu.VMEM((NZ, tokens, C), BF16),
            pltpu.VMEM((C, C), F32),
            pltpu.VMEM((C, C), F32),
            pltpu.VMEM((C, C), F32),
            pltpu.VMEM((1, NS), jnp.int32),
            dma((13,)),
            pltpu.VMEM((1, 128), jnp.int32),
            pltpu.VMEM((CHIPS, 1, 128), jnp.int32),
            pltpu.VMEM((CHIPS, 1, 128), jnp.int32),
            pltpu.VMEM((2, CHIPS, 128), jnp.int32),
            pltpu.VMEM((OWNERS * SLOT_ROWS, C), BF16),
            pltpu.VMEM((OWNERS // 2, 2, 2, SLOT_ROWS, C), BF16),
            pltpu.VMEM((CHIPS, 2, 2, SLOT_ROWS, C), BF16),
            pltpu.VMEM((CHIPS, 2, SLOT_ROWS, C), BF16),
            pltpu.VMEM((OWNERS // 2, 2, SLOT_ROWS, C), BF16),
            pltpu.VMEM((CHIPS, 2, SLOT_ROWS, C), BF16),
            pltpu.VMEM((CHIPS, SLOT_ROWS, C), BF16),
            pltpu.VMEM((C, C), BF16),
            pltpu.VMEM((2, C // 2, C), BF16),
            pltpu.VMEM((2, C, C), BF16),
            pltpu.VMEM((2, C, C), BF16),
            pltpu.VMEM((2, C, C), BF16),
            pltpu.VMEM((2, C, C), BF16),
            pltpu.VMEM((2, C, C), BF16),
            pltpu.VMEM((2, C, C), BF16),
            pltpu.VMEM((5, C, C), F32),
            pltpu.VMEM((C, C), BF16),
            pltpu.VMEM((C, C), BF16),
            pltpu.VMEM(moved, F32),
            pltpu.VMEM(moved, F32),
            dma((1,)),
            dma((SUBS,)),
            dma((SUBS,)),
            dma((SUBS,)),
            dma((SUBS,)),
            dma((SUBS, len(CROSS))),
            dma((SUBS,)),
            dma((9,)),
            dma((SUBS,)),
            dma((SUBS,)),
            dma((SUBS,)),
            dma((3,)),
            dma((3,)),
            dma((3,)),
            dma((3,)),
            dma((3,)),
        ],
        compiler_params=pltpu.CompilerParams(
            collective_id=0, has_side_effects=True, vmem_limit_bytes=40 * 2**20
        ),
        name="exchange",
    )(
        *[
            pltpu.with_memory_space_constraint(operand, pltpu.HBM)
            for operand in (
                activations, cotangent, master, adamw_first_moment, second_moment,
                new_owner.reshape(1, NS),
            )
        ]
    )
    weights, mas, fir, sec = pl.pallas_call(
        store_kernel,
        out_shape=(
            jax.ShapeDtypeStruct((C, NS * C), BF16),
            jax.ShapeDtypeStruct(moved, F32),
            jax.ShapeDtypeStruct(moved, F32),
            jax.ShapeDtypeStruct(moved, F32),
        ),
        in_specs=[vmem] * 4,
        out_specs=[anywhere] * 4,
        scratch_shapes=[
            pltpu.VMEM(moved, F32),
            pltpu.SMEM((2, CHIPS, 128), jnp.int32),
            dma((NS + 4,)),
        ],
        compiler_params=pltpu.CompilerParams(vmem_limit_bytes=8 * 2**20),
        name="store",
    )(
        *[
            pltpu.with_memory_space_constraint(operand, pltpu.VMEM)
            for operand in (gathered, where, fir, sec)
        ]
    )
    out_shape = (1, 1, NS, 2, SLOT_ROWS // 2, C)
    return (weights, mas.reshape(out_shape), fir.reshape(out_shape), sec.reshape(out_shape))


def solution(mesh):
    in_specs = (
        P("dp", "shard"),
        P("dp", None),
        P("dp", "shard"),
        P("dp", "shard"),
        P("dp", "shard"),
        P("dp", "shard", None),
    )
    out_specs = (
        P("dp", None),
        P("dp", "shard", None, None, None, None),
        P("dp", "shard", None, None, None, None),
        P("dp", "shard", None, None, None, None),
    )
    return jax.shard_map(shards, mesh=mesh, in_specs=in_specs, out_specs=out_specs, check_vma=False)
```

time: 46.4 us -> 44.8 us (0.966)
  Pallas kernels: 45.7 us -> 44.1 us
    pallas_call x1, Pallas kernels: 42.9 us -> 41.3 us  [shards(): pl.pallas_call(exchange_kernel, out_shape=(pltpu.VMEM((CHIPS, 2, C, C), B...]
where the time goes in v3:
time: 44.8 us; the launch traced here: 44.7 us
  Pallas kernels  44.1 us (98%)
  between operations  0.64 us (1%)
    pallas_call x1, Pallas kernels, shards(): pl.pallas_call(exchange_kernel, out_shape=(pltpu.VMEM((CHIPS, 2, C, C), B...  41.3 us
    pallas_call x1, Pallas kernels, shards(): pl.pallas_call(store_kernel, out_shape=(jax.ShapeDtypeStruct((C, NS * C),...  2.8 us

profile of v3, /device:TPU:1, one launch (start us, length us, event | category | flops | bytes accessed | tf_op | source)
XLA Modules:
  0.0 44.7 jit_solution(13031954548522889801)
XLA Ops:
  0.6 41.3 %exchange.1 = (bf16[16,2,256,256]{3,2,1,0:T(8,128)(2,1)S(1)}, s32[2,16,128]{2,1,0:T(8,128)S(1)}, f32[32,16,256]{2,1,0:T(8,128)S(1)}, f32[32,16,256]{2,1,0:T(8,128)S(1)}) custom-call(bf16[1024,256]{1,0:T(8,128)(2,1)} %act_hbm.1, bf16[1024,2048]{1,0:T(8,128)(2,1)} %cot_hbm.1, f32[256,256]{1,0:T(8,128)} %mas_hbm.1, f32[256,256]{1,0:T(8,128)} %fir_hbm.1, ...), custom_call_target="tpu_custom_call" | custom-call | tf_op jit(solution)/shard_map/exchange/pallas_call | solution.py:498
  41.9 2.8 %store.1 = (bf16[256,8192]{1,0:T(8,128)(2,1)}, f32[32,16,256]{2,1,0:T(8,128)}, f32[32,16,256]{2,1,0:T(8,128)}, f32[32,16,256]{2,1,0:T(8,128)}) custom-call(bf16[16,2,256,256]{3,2,1,0:T(8,128)(2,1)S(1)} %get-tuple-element.12.w_ref, s32[2,16,128]{2,1,0:T(8,128)S(1)} %get-tuple-element.13.where_ref, f32[32,16,256]{2,1,0:T(8,128)S(1)} %get-tuple-element.14.fir_ref, ...), custom_call_target="tpu_custom_call" | custom-call | tf_op jit(solution)/shard_map/store/pallas_call | solution.py:570

commit v4 on v3

--- a/solution.py
+++ b/solution.py
@@ -17,6 +17,7 @@
 F32 = jnp.float32
 
 NZ = 8
+ORDER = (4, 3, 5, 2, 6, 1, 7, 0)
 NS = 32
 CHIPS = 16
 OWNERS = 28
@@ -25,7 +26,6 @@
 ROWS = (64, 64, 64, 64)
 SUBS = len(ROWS)
 START = tuple(sum(ROWS[:sub]) for sub in range(SUBS))
-DIRECT = 4
 CROSS = ((1, 0), (-1, 0), (0, 1), (0, -1), (2, 0), (0, 2))
 ONWARD = (
     ((0, 1),),
@@ -35,7 +35,6 @@
     ((0, 1), (0, -1)),
     ((1, 0), (-1, 0)),
 )
-FIRST_REST = (0, 1, 2, 3, 4, 6)
 
 
 def moments(adamw_first_moment, second_moment, gradient):
@@ -55,11 +54,11 @@
 def exchange_kernel(
     act_hbm, cot_hbm, mas_hbm, fir_hbm, sec_hbm, own_hbm,
     w_out, where_out, fir_out, sec_out,
-    act, cot, mas, fir, sec, own, load_sem,
+    act, cot, state, own, load_sem,
     own_line, own_land, own_cross, place, pick, st_send, st_land, st_cross, g_send, g_land, g_cross,
     far_send, far_recv, mid_send, mid_recv, near_send, near_recv, two_send, two_recv,
     keep, grad, own_w, new_fir, new_sec,
-    rs_send_sem, first_sem, second_sem, last_sem, ag_send_sem, cross_sem, rest_sem, last_rest_sem, swap_send_sem, swap_sem,
+    rs_send_sem, first_sem, last_sem, ag_send_sem, cross_sem, rest_sem, swap_send_sem, swap_sem,
     own_sem, move_send_sem, move_sem, move_swap_send_sem, move_swap_sem, out_sem,
 ):
     z = lax.axis_index("dp")
@@ -92,20 +91,22 @@
     def await_arrival(ref, sem):
         remote(ref, ref, sem, sem, sibling).wait_recv()
 
-    def cot_load(r):
-        start = pl.multiple_of(at_z(r) * C, C)
-        return pltpu.make_async_copy(cot_hbm.at[:, pl.ds(start, C)], cot.at[r], load_sem.at[r])
-
-    act_load = pltpu.make_async_copy(act_hbm, act, load_sem.at[8])
-    state_loads = [
-        pltpu.make_async_copy(own_hbm, own, load_sem.at[9]),
-        pltpu.make_async_copy(mas_hbm, mas, load_sem.at[10]),
-        pltpu.make_async_copy(fir_hbm, fir, load_sem.at[11]),
-        pltpu.make_async_copy(sec_hbm, sec, load_sem.at[12]),
-    ]
+    def cot_load(slot):
+        start = pl.multiple_of(at_z(ORDER[slot]) * C, C)
+        return pltpu.make_async_copy(
+            cot_hbm.at[:, pl.ds(start, C)], cot.at[slot], load_sem.at[(slot + 1) // 2]
+        )
+
+    def await_cot(slot, count):
+        ref = cot.at[pl.ds(slot, count)]
+        pltpu.make_async_copy(ref, ref, load_sem.at[(slot + 1) // 2]).wait()
+
+    act_load = pltpu.make_async_copy(act_hbm, act, load_sem.at[5])
+    own_load = pltpu.make_async_copy(own_hbm, own, load_sem.at[6])
+    mas, fir, sec = state.at[0], state.at[1], state.at[2]
     act_load.start()
-    for r in (4, 3, 5):
-        cot_load(r).start()
+    for slot in range(3):
+        cot_load(slot).start()
 
     barrier = pltpu.get_barrier_semaphore()
     for step in (1, -1, 2, -2):
@@ -118,22 +119,22 @@
             barrier, inc=1, device_id=on_core(lax.rem(chip + i, CHIPS)), device_id_type=MESH
         )
 
-    def partial(r):
+    def partial(slot):
         return lax.dot_general(
-            cot[r], act[...], (((0,), (0,)), ((), ())), preferred_element_type=F32
+            cot[slot], act[...], (((0,), (0,)), ((), ())), preferred_element_type=F32
         )
 
     act_load.wait()
-    cot_load(4).wait()
-    far_send[...] = partial(4).astype(BF16)
-    cot_load(3).wait()
-    cot_load(5).wait()
-    for load in state_loads:
-        load.start()
-    for r in (2, 6, 1, 7, 0):
-        cot_load(r).start()
-    mid_send[0] = partial(3).astype(BF16)
-    mid_send[1] = partial(5).astype(BF16)
+    await_cot(0, 1)
+    far_send[...] = partial(0).astype(BF16)
+    await_cot(1, 2)
+    own_load.start()
+    for index, src in enumerate((mas_hbm, fir_hbm, sec_hbm)):
+        pltpu.make_async_copy(src, state.at[index], load_sem.at[7]).start()
+    for slot in range(3, NZ):
+        cot_load(slot).start()
+    mid_send[0] = partial(1).astype(BF16)
+    mid_send[1] = partial(2).astype(BF16)
 
     pl.semaphore_wait(barrier, 5 + CHIPS - 1)
 
@@ -158,20 +159,18 @@
             ).start()
 
     def multiply_two():
-        for r in (2, 6):
-            cot_load(r).wait()
-        keep[1] = partial(2)
-        keep[2] = partial(6)
+        await_cot(3, 2)
+        keep[1] = partial(3)
+        keep[2] = partial(4)
 
     def multiply_one():
-        for r in (1, 7):
-            cot_load(r).wait()
-        keep[3] = partial(1)
-        keep[4] = partial(7)
+        await_cot(5, 2)
+        near_send[0] = partial(5).astype(BF16)
+        near_send[1] = partial(6).astype(BF16)
 
     def multiply_own():
-        cot_load(0).wait()
-        keep[0] = partial(0)
+        await_cot(7, 1)
+        keep[0] = partial(7)
 
     def send_near(sub, way):
         remote(
@@ -181,7 +180,6 @@
 
     def reduce_second(sub):
         rows = rows_of(sub)
-        direct = sub < DIRECT
         await_arrival(w_out.at[pl.ds(0, 3), 0, rows], first_sem.at[sub])
         for way in (0, 1):
             both = half_of(sub, way)
@@ -196,21 +194,9 @@
             ).astype(BF16)
             remote(
                 two_send.at[way, rows], two_recv.at[way, rows], rs_send_sem.at[0],
-                last_sem.at[sub] if direct else second_sem.at[sub],
-                (at_z((1 + direct) * (1 - 2 * way)), me),
+                last_sem.at[sub], (at_z(2 - 4 * way), me),
             ).start()
-        if direct:
-            for way in (0, 1):
-                near_send[way, rows] = keep[3 + way, rows].astype(BF16)
-                send_near(sub, way)
-
-    def reduce_third(sub):
-        rows = rows_of(sub)
-        await_arrival(w_out.at[pl.ds(0, 2), 0, rows], second_sem.at[sub])
         for way in (0, 1):
-            near_send[way, rows] = (
-                keep[3 + way, rows] + two_recv[way, rows].astype(F32)
-            ).astype(BF16)
             send_near(sub, way)
 
     def packed(values):
@@ -221,8 +207,8 @@
         )
 
     def pack_state():
-        for load in state_loads:
-            load.wait()
+        own_load.wait()
+        pltpu.make_async_copy(state, state, load_sem.at[7]).wait()
         own_line[...] = jnp.full_like(own_line, -1)
         own_line[:, 0:NS] = own[...]
         move_out(own_line, own_land, 2, lambda to: own_line)
@@ -285,21 +271,18 @@
 
     def gather_send(sub, src, source, to, sem, rows=None):
         dst = w_out.at[source, core, rows_of(sub) if rows is None else rows]
-        remote(dst if src is None else src, dst, ag_send_sem.at[sub], sem, on_core(to)).start()
+        remote(dst if src is None else src, dst, ag_send_sem.at[0], sem, on_core(to)).start()
 
     def update(sub):
         rows = rows_of(sub)
-        direct = sub < DIRECT
-        await_arrival(w_out.at[pl.ds(0, 2 + 2 * direct), 0, rows], last_sem.at[sub])
+        await_arrival(w_out.at[pl.ds(0, 4), 0, rows], last_sem.at[sub])
         total = keep[0, rows]
         for way in (0, 1):
-            total = total + near_recv[way, rows].astype(F32)
-            if direct:
-                total = total + two_recv[way, rows].astype(F32)
+            total = total + near_recv[way, rows].astype(F32) + two_recv[way, rows].astype(F32)
         new_master = adam_update(mas[rows], fir[rows], sec[rows], total)
         own_w[rows] = new_master.astype(BF16)
         for index, (dx, dy) in enumerate(CROSS):
-            gather_send(sub, own_w.at[rows], chip, plane(dx, dy), cross_sem.at[sub, index])
+            gather_send(sub, own_w.at[rows], chip, plane(dx, dy), cross_sem.at[sub, min(index, 4)])
         pltpu.make_async_copy(own_w.at[rows], w_out.at[chip, core, rows], own_sem.at[sub]).start()
         if sub == SUBS - 1:
             swap_one(chip, own_w.at[rows])
@@ -308,26 +291,27 @@
     def forward(sub):
         for index, (dx, dy) in enumerate(CROSS):
             source = plane(-dx, -dy)
-            await_arrival(w_out.at[source, core, rows_of(sub)], cross_sem.at[sub, index])
-            for order, (tx, ty) in enumerate(ONWARD[index]):
-                gather_send(
-                    sub, None, source, plane(tx, ty), rest_arrival(sub, FIRST_REST[index] + order)
-                )
+            if index < 4:
+                await_arrival(w_out.at[source, core, rows_of(sub)], cross_sem.at[sub, index])
+            elif index == 4:
+                await_arrival(w_out.at[pl.ds(0, 2), core, rows_of(sub)], cross_sem.at[sub, 4])
+            for tx, ty in ONWARD[index]:
+                gather_send(sub, None, source, plane(tx, ty), rest_arrival(sub, index // 4))
             if index >= 4:
                 gather_send(
-                    sub, None, source, plane(dy, dx), rest_arrival(sub, 8), half_of(sub, index - 4)
+                    sub, None, source, plane(dy, dx), rest_arrival(sub, 2), half_of(sub, index - 4)
                 )
             if sub == SUBS - 1:
                 swap_one(source)
 
     def rest_arrival(sub, order):
-        return last_rest_sem.at[order] if sub == SUBS - 1 else rest_sem.at[sub]
+        return rest_sem.at[sub + order if sub == SUBS - 1 else sub]
 
     def swap_one(source, src=None):
         sub = SUBS - 1
         dst = w_out.at[source, core, rows_of(sub)]
         remote(
-            dst if src is None else src, dst, swap_send_sem.at[sub], swap_sem.at[sub], sibling
+            dst if src is None else src, dst, swap_send_sem.at[0], swap_sem.at[0], sibling
         ).start()
 
     def swap(sub):
@@ -336,24 +320,22 @@
             await_arrival(w_out.at[pl.ds(0, 9), 0, rows], rest_sem.at[sub])
             pltpu.make_async_copy(own_w.at[rows], w_out.at[chip, core, rows], own_sem.at[sub]).wait()
             half = w_out.at[:, core, rows]
-            remote(half, half, swap_send_sem.at[sub], swap_sem.at[sub], sibling).start()
+            remote(half, half, swap_send_sem.at[0], swap_sem.at[0], sibling).start()
             return
         for index, (dx, dy) in enumerate(CROSS):
-            for order, (tx, ty) in enumerate(ONWARD[index]):
-                source = plane(-dx - tx, -dy - ty)
-                await_arrival(
-                    w_out.at[source, core, rows], rest_arrival(sub, FIRST_REST[index] + order)
-                )
-                swap_one(source)
+            if index in (0, 4):
+                await_arrival(w_out.at[pl.ds(0, 4), core, rows], rest_arrival(sub, index // 4))
+            for tx, ty in ONWARD[index]:
+                swap_one(plane(-dx - tx, -dy - ty))
         source = plane(2, 2)
-        await_arrival(w_out.at[source, core, rows], rest_arrival(sub, 8))
+        await_arrival(w_out.at[source, core, rows], rest_arrival(sub, 2))
         swap_one(source)
         pltpu.make_async_copy(own_w.at[rows], w_out.at[chip, core, rows], own_sem.at[sub]).wait()
 
-    def settle(sub):
-        await_arrival(w_out.at[:, 1 - core, rows_of(sub)], swap_sem.at[sub])
-        await_sent(w_out.at[:, core, rows_of(sub)], swap_send_sem.at[sub])
-        await_sent(w_out.at[pl.ds(0, 15), 0, rows_of(sub)], ag_send_sem.at[sub])
+    def settle():
+        await_arrival(w_out.at[:, 1 - core], swap_sem.at[0])
+        await_sent(w_out.at[:, core], swap_send_sem.at[0])
+        await_sent(w_out.at[pl.ds(0, 15), core], ag_send_sem.at[0])
 
     def send_gradient():
         g_send[...] = packed(grad[...])
@@ -428,15 +410,12 @@
     forward(3)
     pl.when(core == 1)(send_gradient)
     swap(1)
+    find_places()
     move_across(g_land, g_cross, 1)
     swap(2)
     swap(3)
-    find_places()
     own_blocks()
-    settle(0)
-    settle(1)
-    settle(2)
-    settle(3)
+    settle()
 
     await_sent(w_out.at[pl.ds(0, 7), 0], rs_send_sem.at[0])
     pltpu.make_async_copy(new_fir, fir_out, out_sem.at[0]).wait()
@@ -456,17 +435,19 @@
     w_ref, where_ref, fir_ref, sec_ref, weights, out_mas, out_fir, out_sec, new_mas, places, sem
 ):
     core = lax.rem(lax.axis_index("shard"), 2)
-    where_copy = pltpu.make_async_copy(where_ref, places, sem.at[NS])
+    where_copy = pltpu.make_async_copy(where_ref, places, sem.at[1])
     where_copy.start()
     copies = [
         pltpu.make_async_copy(
-            w_ref.at[s // 2, s % 2], weights.at[:, pl.ds(s * C, C)], sem.at[s]
+            w_ref.at[s // 2, s % 2], weights.at[:, pl.ds(s * C, C)], sem.at[0]
         )
         for s in range(NS)
     ]
-    copies.append(pltpu.make_async_copy(fir_ref, out_fir, sem.at[NS + 1]))
-    copies.append(pltpu.make_async_copy(sec_ref, out_sec, sem.at[NS + 2]))
-    for copy in copies:
+    moved = [
+        pltpu.make_async_copy(fir_ref, out_fir, sem.at[2]),
+        pltpu.make_async_copy(sec_ref, out_sec, sem.at[3]),
+    ]
+    for copy in copies + moved:
         copy.start()
 
     where_copy.wait()
@@ -483,10 +464,11 @@
                 rows = jnp.where(lax.rem(held, 2) == 1, tile[8:16], tile[0:8])
                 new_mas[source * 2 + side, pl.ds(slot * 8, 8)] = jnp.where(block >= 0, rows, 0.0)
 
-    copies.append(pltpu.make_async_copy(new_mas, out_mas, sem.at[NS + 3]))
-    copies[-1].start()
-    for copy in copies:
+    moved.append(pltpu.make_async_copy(new_mas, out_mas, sem.at[4]))
+    moved[-1].start()
+    for copy in moved:
         copy.wait()
+    pltpu.make_async_copy(weights, weights, sem.at[0]).wait()
 
 
 def shards(activations, cotangent, master, adamw_first_moment, second_moment, new_owner):
@@ -508,11 +490,9 @@
         scratch_shapes=[
             pltpu.VMEM((tokens, C), BF16),
             pltpu.VMEM((NZ, tokens, C), BF16),
-            pltpu.VMEM((C, C), F32),
-            pltpu.VMEM((C, C), F32),
-            pltpu.VMEM((C, C), F32),
+            pltpu.VMEM((3, C, C), F32),
             pltpu.VMEM((1, NS), jnp.int32),
-            dma((13,)),
+            dma((8,)),
             pltpu.VMEM((1, 128), jnp.int32),
             pltpu.VMEM((CHIPS, 1, 128), jnp.int32),
             pltpu.VMEM((CHIPS, 1, 128), jnp.int32),
@@ -532,7 +512,7 @@
             pltpu.VMEM((2, C, C), BF16),
             pltpu.VMEM((2, C, C), BF16),
             pltpu.VMEM((2, C, C), BF16),
-            pltpu.VMEM((5, C, C), F32),
+            pltpu.VMEM((3, C, C), F32),
             pltpu.VMEM((C, C), BF16),
             pltpu.VMEM((C, C), BF16),
             pltpu.VMEM(moved, F32),
@@ -540,13 +520,11 @@
             dma((1,)),
             dma((SUBS,)),
             dma((SUBS,)),
-            dma((SUBS,)),
-            dma((SUBS,)),
-            dma((SUBS, len(CROSS))),
-            dma((SUBS,)),
-            dma((9,)),
-            dma((SUBS,)),
-            dma((SUBS,)),
+            dma((1,)),
+            dma((SUBS, 5)),
+            dma((SUBS + 2,)),
+            dma((1,)),
+            dma((1,)),
             dma((SUBS,)),
             dma((3,)),
             dma((3,)),
@@ -580,7 +558,7 @@
         scratch_shapes=[
             pltpu.VMEM(moved, F32),
             pltpu.SMEM((2, CHIPS, 128), jnp.int32),
-            dma((NS + 4,)),
+            dma((5,)),
         ],
         compiler_params=pltpu.CompilerParams(vmem_limit_bytes=8 * 2**20),
         name="store",

time: 44.8 us -> 44.3 us (0.989)
  Pallas kernels: 44.1 us -> 43.6 us
where the time goes in v4:
time: 44.3 us; the launch traced here: 44.2 us
  Pallas kernels  43.6 us (98%)
  between operations  0.64 us (1%)
    pallas_call x1, Pallas kernels, shards(): pl.pallas_call(exchange_kernel, out_shape=(pltpu.VMEM((CHIPS, 2, C, C), B...  41 us
    pallas_call x1, Pallas kernels, shards(): pl.pallas_call(store_kernel, out_shape=(jax.ShapeDtypeStruct((C, NS * C),...  2.53 us

profile of v4, /device:TPU:1, one launch (start us, length us, event | category | flops | bytes accessed | tf_op | source)
XLA Modules:
  0.0 44.2 jit_solution(9501728171027330513)
XLA Ops:
  0.6 41.0 %exchange.1 = (bf16[16,2,256,256]{3,2,1,0:T(8,128)(2,1)S(1)}, s32[2,16,128]{2,1,0:T(8,128)S(1)}, f32[32,16,256]{2,1,0:T(8,128)S(1)}, f32[32,16,256]{2,1,0:T(8,128)S(1)}) custom-call(bf16[1024,256]{1,0:T(8,128)(2,1)} %act_hbm.1, bf16[1024,2048]{1,0:T(8,128)(2,1)} %cot_hbm.1, f32[256,256]{1,0:T(8,128)} %mas_hbm.1, f32[256,256]{1,0:T(8,128)} %fir_hbm.1, ...), custom_call_target="tpu_custom_call" | custom-call | tf_op jit(solution)/shard_map/exchange/pallas_call | solution.py:480
  41.7 2.5 %store.1 = (bf16[256,8192]{1,0:T(8,128)(2,1)}, f32[32,16,256]{2,1,0:T(8,128)}, f32[32,16,256]{2,1,0:T(8,128)}, f32[32,16,256]{2,1,0:T(8,128)}) custom-call(bf16[16,2,256,256]{3,2,1,0:T(8,128)(2,1)S(1)} %get-tuple-element.12.w_ref, s32[2,16,128]{2,1,0:T(8,128)S(1)} %get-tuple-element.13.where_ref, f32[32,16,256]{2,1,0:T(8,128)S(1)} %get-tuple-element.14.fir_ref, ...), custom_call_target="tpu_custom_call" | custom-call | tf_op jit(solution)/shard_map/store/pallas_call | solution.py:548

commit v5 on v4

--- a/solution.py
+++ b/solution.py
@@ -59,7 +59,7 @@
     far_send, far_recv, mid_send, mid_recv, near_send, near_recv, two_send, two_recv,
     keep, grad, own_w, new_fir, new_sec,
     rs_send_sem, first_sem, last_sem, ag_send_sem, cross_sem, rest_sem, swap_send_sem, swap_sem,
-    own_sem, move_send_sem, move_sem, move_swap_send_sem, move_swap_sem, out_sem,
+    plane_sem, own_sem, move_send_sem, move_sem, move_swap_send_sem, move_swap_sem, out_sem,
 ):
     z = lax.axis_index("dp")
     me = lax.axis_index("shard")
@@ -109,15 +109,11 @@
         cot_load(slot).start()
 
     barrier = pltpu.get_barrier_semaphore()
-    for step in (1, -1, 2, -2):
-        pl.semaphore_signal(barrier, inc=1, device_id=(at_z(step), me), device_id_type=MESH)
-    pl.semaphore_signal(barrier, inc=1, device_id=sibling, device_id_type=MESH)
-
-    @pl.loop(1, CHIPS)
-    def _(i):
-        pl.semaphore_signal(
-            barrier, inc=1, device_id=on_core(lax.rem(chip + i, CHIPS)), device_id_type=MESH
-        )
+    row = [on_core(plane(dx, 0)) for dx in (1, 2, 3)]
+    column = [on_core(plane(0, dy)) for dy in (1, 2, 3)]
+    along_z = [(at_z(step), me) for step in (1, -1, 2, -2)]
+    for partner in along_z + [sibling] + row + column:
+        pl.semaphore_signal(barrier, inc=1, device_id=partner, device_id_type=MESH)
 
     def partial(slot):
         return lax.dot_general(
@@ -127,16 +123,10 @@
     act_load.wait()
     await_cot(0, 1)
     far_send[...] = partial(0).astype(BF16)
-    await_cot(1, 2)
-    own_load.start()
-    for index, src in enumerate((mas_hbm, fir_hbm, sec_hbm)):
-        pltpu.make_async_copy(src, state.at[index], load_sem.at[7]).start()
-    for slot in range(3, NZ):
-        cot_load(slot).start()
-    mid_send[0] = partial(1).astype(BF16)
-    mid_send[1] = partial(2).astype(BF16)
-
-    pl.semaphore_wait(barrier, 5 + CHIPS - 1)
+
+    pl.semaphore_wait(barrier, 11)
+    for partner in row:
+        pl.semaphore_signal(plane_sem, inc=1, device_id=partner, device_id_type=MESH)
 
     def rows_of(sub):
         return pl.ds(START[sub], ROWS[sub])
@@ -147,16 +137,29 @@
     def far_slot(sub):
         return pl.ds(START[sub] // 2, ROWS[sub] // 2)
 
-    def reduce_first(sub):
+    def reduce_far(sub):
         for way in (0, 1):
             remote(
                 far_send.at[half_of(sub, way)], far_recv.at[way, far_slot(sub)],
                 rs_send_sem.at[0], first_sem.at[sub], (at_z(2 - 4 * way), me),
             ).start()
+
+    def reduce_mid(sub):
+        for way in (0, 1):
             remote(
                 mid_send.at[way, rows_of(sub)], mid_recv.at[way, rows_of(sub)],
                 rs_send_sem.at[0], first_sem.at[sub], (at_z(1 - 2 * way), me),
             ).start()
+
+    def multiply_three():
+        await_cot(1, 2)
+        own_load.start()
+        for index, src in enumerate((mas_hbm, fir_hbm, sec_hbm)):
+            pltpu.make_async_copy(src, state.at[index], load_sem.at[7]).start()
+        for slot in range(3, NZ):
+            cot_load(slot).start()
+        mid_send[0] = partial(1).astype(BF16)
+        mid_send[1] = partial(2).astype(BF16)
 
     def multiply_two():
         await_cot(3, 2)
@@ -196,6 +199,8 @@
                 two_send.at[way, rows], two_recv.at[way, rows], rs_send_sem.at[0],
                 last_sem.at[sub], (at_z(2 - 4 * way), me),
             ).start()
+
+    def reduce_near(sub):
         for way in (0, 1):
             send_near(sub, way)
 
@@ -211,7 +216,6 @@
         pltpu.make_async_copy(state, state, load_sem.at[7]).wait()
         own_line[...] = jnp.full_like(own_line, -1)
         own_line[:, 0:NS] = own[...]
-        move_out(own_line, own_land, 2, lambda to: own_line)
         owner = own[...].astype(F32)
         row_id = lax.broadcasted_iota(jnp.int32, (NS, NS), 0)
         col_id = lax.broadcasted_iota(jnp.int32, (NS, NS), 1)
@@ -230,7 +234,9 @@
 
         st_send[:, :, 0] = packed(fir[...].astype(BF16))
         st_send[:, :, 1] = packed(sec[...].astype(BF16))
+        pl.semaphore_wait(plane_sem, 3)
         move_out(st_send, st_land, 0)
+        move_out(own_line, own_land, 2, lambda to: own_line)
 
     def move_out(send, land, index, piece=None):
         if piece is None:
@@ -384,24 +390,33 @@
         pltpu.make_async_copy(new_fir, fir_out, out_sem.at[0]).start()
         pltpu.make_async_copy(new_sec, sec_out, out_sem.at[1]).start()
 
-    reduce_first(0)
-    reduce_first(1)
-    reduce_first(2)
+    reduce_far(0)
+    reduce_far(1)
+    reduce_far(2)
+    multiply_three()
+    reduce_mid(0)
+    reduce_mid(1)
+    reduce_mid(2)
+    multiply_two()
     pack_state()
-    multiply_two()
     multiply_one()
     reduce_second(0)
-    reduce_first(3)
+    reduce_near(0)
+    reduce_far(3)
+    reduce_mid(3)
     multiply_own()
     reduce_second(1)
+    reduce_near(1)
     reduce_second(2)
+    reduce_near(2)
     update(0)
     reduce_second(3)
+    reduce_near(3)
     update(1)
     forward(0)
     update(2)
+    update(3)
     forward(1)
-    update(3)
     pl.when(core == 0)(send_gradient)
     forward(2)
     move_across(own_land, own_cross, 2)
@@ -525,6 +540,7 @@
             dma((SUBS + 2,)),
             dma((1,)),
             dma((1,)),
+            pltpu.SemaphoreType.REGULAR,
             dma((SUBS,)),
             dma((3,)),
             dma((3,)),

time: 44.3 us -> 43.7 us (0.986)
  Pallas kernels: 43.6 us -> 43 us
    pallas_call x1, Pallas kernels: 41 us -> 40.5 us  [shards(): pl.pallas_call(exchange_kernel, out_shape=(pltpu.VMEM((CHIPS, 2, C, C), B...]
where the time goes in v5:
time: 43.7 us; the launch traced here: 43.6 us
  Pallas kernels  43 us (98%)
  between operations  0.64 us (1%)
    pallas_call x1, Pallas kernels, shards(): pl.pallas_call(exchange_kernel, out_shape=(pltpu.VMEM((CHIPS, 2, C, C), B...  40.5 us
    pallas_call x1, Pallas kernels, shards(): pl.pallas_call(store_kernel, out_shape=(jax.ShapeDtypeStruct((C, NS * C),...  2.53 us

profile of v5, /device:TPU:1, one launch (start us, length us, event | category | flops | bytes accessed | tf_op | source)
XLA Modules:
  0.0 43.6 jit_solution(14062352940018575384)
XLA Ops:
  0.6 40.5 %exchange.1 = (bf16[16,2,256,256]{3,2,1,0:T(8,128)(2,1)S(1)}, s32[2,16,128]{2,1,0:T(8,128)S(1)}, f32[32,16,256]{2,1,0:T(8,128)S(1)}, f32[32,16,256]{2,1,0:T(8,128)S(1)}) custom-call(bf16[1024,256]{1,0:T(8,128)(2,1)} %act_hbm.1, bf16[1024,2048]{1,0:T(8,128)(2,1)} %cot_hbm.1, f32[256,256]{1,0:T(8,128)} %mas_hbm.1, f32[256,256]{1,0:T(8,128)} %fir_hbm.1, ...), custom_call_target="tpu_custom_call" | custom-call | tf_op jit(solution)/shard_map/exchange/pallas_call | solution.py:495
  41.1 2.5 %store.1 = (bf16[256,8192]{1,0:T(8,128)(2,1)}, f32[32,16,256]{2,1,0:T(8,128)}, f32[32,16,256]{2,1,0:T(8,128)}, f32[32,16,256]{2,1,0:T(8,128)}) custom-call(bf16[16,2,256,256]{3,2,1,0:T(8,128)(2,1)S(1)} %get-tuple-element.12.w_ref, s32[2,16,128]{2,1,0:T(8,128)S(1)} %get-tuple-element.13.where_ref, f32[32,16,256]{2,1,0:T(8,128)S(1)} %get-tuple-element.14.fir_ref, ...), custom_call_target="tpu_custom_call" | custom-call | tf_op jit(solution)/shard_map/store/pallas_call | solution.py:564

commit v6 on v5

--- a/solution.py
+++ b/solution.py
@@ -288,7 +288,7 @@
         new_master = adam_update(mas[rows], fir[rows], sec[rows], total)
         own_w[rows] = new_master.astype(BF16)
         for index, (dx, dy) in enumerate(CROSS):
-            gather_send(sub, own_w.at[rows], chip, plane(dx, dy), cross_sem.at[sub, min(index, 4)])
+            gather_send(sub, own_w.at[rows], chip, plane(dx, dy), cross_sem.at[sub, index // 4])
         pltpu.make_async_copy(own_w.at[rows], w_out.at[chip, core, rows], own_sem.at[sub]).start()
         if sub == SUBS - 1:
             swap_one(chip, own_w.at[rows])
@@ -297,10 +297,11 @@
     def forward(sub):
         for index, (dx, dy) in enumerate(CROSS):
             source = plane(-dx, -dy)
-            if index < 4:
-                await_arrival(w_out.at[source, core, rows_of(sub)], cross_sem.at[sub, index])
-            elif index == 4:
-                await_arrival(w_out.at[pl.ds(0, 2), core, rows_of(sub)], cross_sem.at[sub, 4])
+            if index in (0, 4):
+                count = 4 - index // 2
+                await_arrival(
+                    w_out.at[pl.ds(0, count), core, rows_of(sub)], cross_sem.at[sub, index // 4]
+                )
             for tx, ty in ONWARD[index]:
                 gather_send(sub, None, source, plane(tx, ty), rest_arrival(sub, index // 4))
             if index >= 4:
@@ -536,7 +537,7 @@
             dma((SUBS,)),
             dma((SUBS,)),
             dma((1,)),
-            dma((SUBS, 5)),
+            dma((SUBS, 2)),
             dma((SUBS + 2,)),
             dma((1,)),
             dma((1,)),

time: 43.7 us -> 43.6 us (level)
  no operation moved by 1% of the time
where the time goes in v6:
time: 43.6 us; the launch traced here: 43.5 us
  Pallas kernels  42.9 us (98%)
  between operations  0.64 us (1%)
    pallas_call x1, Pallas kernels, shards(): pl.pallas_call(exchange_kernel, out_shape=(pltpu.VMEM((CHIPS, 2, C, C), B...  40.4 us
    pallas_call x1, Pallas kernels, shards(): pl.pallas_call(store_kernel, out_shape=(jax.ShapeDtypeStruct((C, NS * C),...  2.53 us

profile of v6, /device:TPU:1, one launch (start us, length us, event | category | flops | bytes accessed | tf_op | source)
XLA Modules:
  0.0 43.5 jit_solution(17640830561500510249)
XLA Ops:
  0.6 40.4 %exchange.1 = (bf16[16,2,256,256]{3,2,1,0:T(8,128)(2,1)S(1)}, s32[2,16,128]{2,1,0:T(8,128)S(1)}, f32[32,16,256]{2,1,0:T(8,128)S(1)}, f32[32,16,256]{2,1,0:T(8,128)S(1)}) custom-call(bf16[1024,256]{1,0:T(8,128)(2,1)} %act_hbm.1, bf16[1024,2048]{1,0:T(8,128)(2,1)} %cot_hbm.1, f32[256,256]{1,0:T(8,128)} %mas_hbm.1, f32[256,256]{1,0:T(8,128)} %fir_hbm.1, ...), custom_call_target="tpu_custom_call" | custom-call | tf_op jit(solution)/shard_map/exchange/pallas_call | solution.py:496
  41.0 2.5 %store.1 = (bf16[256,8192]{1,0:T(8,128)(2,1)}, f32[32,16,256]{2,1,0:T(8,128)}, f32[32,16,256]{2,1,0:T(8,128)}, f32[32,16,256]{2,1,0:T(8,128)}) custom-call(bf16[16,2,256,256]{3,2,1,0:T(8,128)(2,1)S(1)} %get-tuple-element.12.w_ref, s32[2,16,128]{2,1,0:T(8,128)S(1)} %get-tuple-element.13.where_ref, f32[32,16,256]{2,1,0:T(8,128)S(1)} %get-tuple-element.14.fir_ref, ...), custom_call_target="tpu_custom_call" | custom-call | tf_op jit(solution)/shard_map/store/pallas_call | solution.py:565
